TPU v7x, 32 devices: a whole 2x2x4 slice. The times are simulated.
32 devices in a mesh: seq: 8 (over y, x, core), emb: 4 (over z).
Axes of the slice: x: 2, y: 2, z: 4, core: 2. Of those that a mesh axis runs over, the one named last changes fastest.
Arguments:
- source: bfloat16 [8192, 1024], P('seq', 'emb'), may hold values from -6 to 6
- target: bfloat16 [8192, 1024], P('seq', 'emb'), may hold values from -6 to 6
- doc_ids: int32 [8192], replicated, may hold values from 0 to 127, never falling along the last dimension, each value on 1 to 512 neighbouring positions
- offsets: int32 [128], P(('seq', 'emb')), may hold values from -2048 to 2048, as said below
Outputs:
- projected: bfloat16 [8192, 1024], P('seq', 'emb')
- row_mass: float32 [8192], P(('seq', 'emb'))
Inputs may be any that keep to these rules, and one draw needn't show every extreme that they name: doc_ids never fall along the sentences. `offsets`: both ends of the range occur in every draw.
All inputs are finite; a program needn't handle non-finite values.
Results may differ from a plain program's by a relative error of at most 0.006.
Values may be sent and summed in bfloat16 or wider, within the bound.
A program may use at most 128 MiB of HBM per device.

v0:
```python
import jax
import jax.numpy as jnp
from jax import lax
from jax.sharding import PartitionSpec as P

BAND = 2048
OFFSET_BLOCK = 64
ITERS = 3


INV_EPS = 50.0
PENALTY = 0.04


def shifted_2(block, axis, distance):
    devices = range(lax.axis_size(axis))
    route = [(i - distance, i) for i in devices if i - distance in devices]
    return lax.ppermute(block, axis, route)


def per_device(source, target, doc_ids, offsets):
    n_emb = lax.axis_size("emb")
    rows_dev = source.shape[0] // n_emb
    place = lax.axis_index(("seq", "emb"))
    sentences = doc_ids.shape[0]
    reach = 2 * BAND
    hops = reach // rows_dev
    width = rows_dev + 2 * reach
    src_rows, tgt_rows = (
        lax.all_to_all(source, "emb", split_axis=0, concat_axis=1, tiled=True),
        lax.all_to_all(target, "emb", split_axis=0, concat_axis=1, tiled=True),
    )
    lower = {}
    upper = {}
    for dist in range(1, hops + 1):
        for sign in (1, -1):
            moved = shifted_2(tgt_rows, ("seq", "emb"), -sign * dist)
            if sign > 0:
                upper[dist] = moved
            else:
                lower[dist] = moved
    pieces = (
        [lower[dist] for dist in range(hops, 0, -1)]
        + [tgt_rows]
        + [upper[dist] for dist in range(1, hops + 1)]
    )
    window = jnp.concatenate(pieces, axis=0)
    src_scale = lax.rsqrt(jnp.sum(jnp.square(src_rows.astype(jnp.float32)), axis=1) + 1e-06)
    tgt_scale = lax.rsqrt(jnp.sum(jnp.square(window.astype(jnp.float32)), axis=1) + 1e-06)
    first_row = place * rows_dev
    src_pos = first_row + jnp.arange(rows_dev, dtype=jnp.int32)
    tgt_pos = first_row - reach + jnp.arange(width, dtype=jnp.int32)
    valid = (tgt_pos >= 0) & (tgt_pos < sentences)
    shifted = jnp.repeat(offsets, OFFSET_BLOCK)
    band = (jnp.abs(tgt_pos[None, :] - src_pos[:, None] - shifted[:, None]) <= BAND) & valid[
        None, :
    ]
    pad_docs = jnp.pad(doc_ids, (reach, reach), constant_values=-1)
    same = (
        lax.dynamic_slice_in_dim(doc_ids, first_row, rows_dev, 0)[:, None]
        == lax.dynamic_slice_in_dim(pad_docs, first_row, width, 0)[None, :]
    )
    penalty = jnp.where(same, 0.0, PENALTY)

    def cosines():
        dots = lax.dot_general(
            src_rows, window, (((1,), (1,)), ((), ())), preferred_element_type=jnp.float32
        )
        return dots * src_scale[:, None] * tgt_scale[None, :]

    def to_kernel(cosine):
        return jnp.where(band, jnp.exp((cosine - penalty) * INV_EPS), 0.0)

    def kernel():
        return to_kernel(cosines())

    scaling = valid.astype(jnp.float32)
    inverse = jnp.zeros((rows_dev,), jnp.float32)
    for step in range(ITERS):
        kern = kernel()
        inverse = 1.0 / jnp.sum(kern * scaling[None, :], axis=1)
        part = jnp.sum(kern * inverse[:, None], axis=0)
        owned = part[reach : reach + rows_dev]
        for lag in range(-hops, hops + 1):
            if lag != 0:
                begin = reach + lag * rows_dev
                owned = owned + shifted_2(part[begin : begin + rows_dev], ("seq", "emb"), lag)
        own_scaling = 1.0 / owned
        parts_list = []
        for lag in range(-hops, hops + 1):
            if lag == 0:
                parts_list.append(own_scaling)
            else:
                parts_list.append(shifted_2(own_scaling, ("seq", "emb"), -lag))
        scaling = jnp.concatenate(parts_list, axis=0)
    kern = kernel()
    totals = jnp.sum(kern * scaling[None, :], axis=1)
    row_mass = inverse * totals
    weights = (kern * scaling[None, :] / totals[:, None]).astype(jnp.bfloat16)
    mixed = jnp.dot(weights, window, preferred_element_type=jnp.float32).astype(jnp.bfloat16)
    projected = lax.all_to_all(mixed, "emb", split_axis=1, concat_axis=0, tiled=True)
    return (projected, row_mass)


def solution(mesh):
    in_specs = (P("seq", "emb"), P("seq", "emb"), P(), P(("seq", "emb")))
    out_specs = (P("seq", "emb"), P(("seq", "emb")))
    return jax.shard_map(
        per_device, mesh=mesh, in_specs=in_specs, out_specs=out_specs, check_vma=False
    )
```

profile of v0, /device:TPU:0, one launch (start us, length us, event | category | flops | bytes accessed | tf_op | source)
XLA Modules:
  0.0 957.7 jit_solution(12733945937025245151)
XLA Ops:
  0.6 20.8 %all_to_all.57 = bf16[4,256,256]{2,1,0:T(8,128)(2,1)S(1)} all-to-all(bf16[4,256,256]{2,1,0:T(8,128)(2,1)} %bitcast.63), channel_id=1, replica_groups=mesh['seq'=8,'emb'=4] {'emb'}, dimensions={0} | all-to-all | bytes 1048576 | tf_op jit(solution)/shard_map/all_to_all | solution.py:31
  21.4 3.5 all-to-all-start.1
  26.0 4.2 collective-permute-start
  30.2 4.4 collective-permute-start.1
  42.5 16.1 %collective-permute-done = bf16[256,1024]{0,1:T(8,128)(2,1)} collective-permute-done((bf16[256,1024]{0,1:T(8,128)(2,1)S(1)}, bf16[256,1024]{0,1:T(8,128)(2,1)}, u32[]{:S(2)}, u32[]{:S(2)}) %collective-permute-start) | collective-permute-done | bytes 524320 | tf_op jit(solution)/shard_map/ppermute | solution.py:18
  58.6 8.6 collective-permute-start.5
  68.3 13.8 %collective-permute-start.6 = (bf16[256,1024]{0,1:T(8,128)(2,1)S(1)}, bf16[256,1024]{0,1:T(8,128)(2,1)S(1)}, u32[]{:S(2)}, u32[]{:S(2)}) collective-permute-start(bf16[256,1024]{0,1:T(8,128)(2,1)S(1)} %bitcast.34), channel_id=1, source_target_pairs={{0,10},{1,11},{2,12},{3,13},{4,14},{5,15},{6,16},{7,17},{8,18},{9,... | collective-permute-start | bytes 1572872 | tf_op jit(solution)/shard_map/ppermute | solution.py:18
  82.2 13.1 %collective-permute-start.7 = (bf16[256,1024]{0,1:T(8,128)(2,1)S(1)}, bf16[256,1024]{0,1:T(8,128)(2,1)S(1)}, u32[]{:S(2)}, u32[]{:S(2)}) collective-permute-start(bf16[256,1024]{0,1:T(8,128)(2,1)S(1)} %bitcast.35), channel_id=1, source_target_pairs={{0,9},{1,10},{2,11},{3,12},{4,13},{5,14},{6,15},{7,16},{8,17},{9,1... | collective-permute-start | bytes 1572872 | tf_op jit(solution)/shard_map/ppermute | solution.py:18
  96.4 3.4 collective-permute-start.8
  99.9 8.6 collective-permute-start.9
  108.6 19.7 %collective-permute-start.10 = (bf16[256,1024]{0,1:T(8,128)(2,1)S(1)}, bf16[256,1024]{0,1:T(8,128)(2,1)S(1)}, u32[]{:S(2)}, u32[]{:S(2)}) collective-permute-start(bf16[256,1024]{0,1:T(8,128)(2,1)S(1)} %bitcast.38), channel_id=1, source_target_pairs={{0,6},{1,7},{2,8},{3,9},{4,10},{5,11},{6,12},{7,13},{8,14},{9,15},... | collective-permute-start | bytes 1572872 | tf_op jit(solution)/shard_map/ppermute | solution.py:18
  128.3 14.1 %collective-permute-start.11 = (bf16[256,1024]{0,1:T(8,128)(2,1)S(1)}, bf16[256,1024]{0,1:T(8,128)(2,1)S(1)}, u32[]{:S(2)}, u32[]{:S(2)}) collective-permute-start(bf16[256,1024]{0,1:T(8,128)(2,1)S(1)} %bitcast.39), channel_id=1, source_target_pairs={{0,5},{1,6},{2,7},{3,8},{4,9},{5,10},{6,11},{7,12},{8,13},{9,14},{... | collective-permute-start | bytes 1572872 | tf_op jit(solution)/shard_map/ppermute | solution.py:18
  143.8 24.5 %collective-permute-start.13 = (bf16[256,1024]{0,1:T(8,128)(2,1)S(1)}, bf16[256,1024]{0,1:T(8,128)(2,1)S(1)}, u32[]{:S(2)}, u32[]{:S(2)}) collective-permute-start(bf16[256,1024]{0,1:T(8,128)(2,1)S(1)} %bitcast.41), channel_id=1, source_target_pairs={{0,3},{1,4},{2,5},{3,6},{4,7},{5,8},{6,9},{7,10},{8,11},{9,12},{10... | collective-permute-start | bytes 1572872 | tf_op jit(solution)/shard_map/ppermute | solution.py:18
  168.4 8.1 collective-permute-start.14
  182.0 9.8 %collective-permute-done.14 = bf16[256,1024]{0,1:T(8,128)(2,1)S(1)} collective-permute-done((bf16[256,1024]{0,1:T(8,128)(2,1)S(1)}, bf16[256,1024]{0,1:T(8,128)(2,1)S(1)}, u32[]{:S(2)}, u32[]{:S(2)}) %collective-permute-start.14) | collective-permute-done | bytes 524320 | tf_op jit(solution)/shard_map/ppermute | solution.py:18
  193.2 9.9 %collective-permute-done.15 = bf16[256,1024]{0,1:T(8,128)(2,1)S(1)} collective-permute-done((bf16[256,1024]{0,1:T(8,128)(2,1)S(1)}, bf16[256,1024]{0,1:T(8,128)(2,1)S(1)}, u32[]{:S(2)}, u32[]{:S(2)}) %collective-permute-start.15) | collective-permute-done | bytes 524320 | tf_op jit(solution)/shard_map/ppermute | solution.py:18
  204.5 22.4 %collective-permute-done.16 = bf16[256,1024]{0,1:T(8,128)(2,1)S(1)} collective-permute-done((bf16[256,1024]{0,1:T(8,128)(2,1)S(1)}, bf16[256,1024]{0,1:T(8,128)(2,1)S(1)}, u32[]{:S(2)}, u32[]{:S(2)}) %collective-permute-start.16) | collective-permute-done | bytes 524320 | tf_op jit(solution)/shard_map/ppermute | solution.py:18
  228.2 53.7 %collective-permute-done.17 = bf16[256,1024]{0,1:T(8,128)(2,1)S(1)} collective-permute-done((bf16[256,1024]{0,1:T(8,128)(2,1)S(1)}, bf16[256,1024]{0,1:T(8,128)(2,1)S(1)}, u32[]{:S(2)}, u32[]{:S(2)}) %collective-permute-start.17) | collective-permute-done | bytes 524320 | tf_op jit(solution)/shard_map/ppermute | solution.py:18
  287.3 10.4 %collective-permute-done.21 = bf16[256,1024]{0,1:T(8,128)(2,1)S(1)} collective-permute-done((bf16[256,1024]{0,1:T(8,128)(2,1)S(1)}, bf16[256,1024]{0,1:T(8,128)(2,1)S(1)}, u32[]{:S(2)}, u32[]{:S(2)}) %collective-permute-start.21) | collective-permute-done | bytes 524320 | tf_op jit(solution)/shard_map/ppermute | solution.py:18
  300.4 23.3 %collective-permute-done.23 = bf16[256,1024]{0,1:T(8,128)(2,1)S(1)} collective-permute-done((bf16[256,1024]{0,1:T(8,128)(2,1)S(1)}, bf16[256,1024]{0,1:T(8,128)(2,1)S(1)}, u32[]{:S(2)}, u32[]{:S(2)}) %collective-permute-start.23) | collective-permute-done | bytes 524320 | tf_op jit(solution)/shard_map/ppermute | solution.py:18
  326.4 35.6 %collective-permute-done.25 = bf16[256,1024]{0,1:T(8,128)(2,1)S(1)} collective-permute-done((bf16[256,1024]{0,1:T(8,128)(2,1)S(1)}, bf16[256,1024]{0,1:T(8,128)(2,1)S(1)}, u32[]{:S(2)}, u32[]{:S(2)}) %collective-permute-start.25) | collective-permute-done | bytes 524320 | tf_op jit(solution)/shard_map/ppermute | solution.py:18
  364.8 13.0 %collective-permute-done.29 = bf16[256,1024]{0,1:T(8,128)(2,1)S(1)} collective-permute-done((bf16[256,1024]{0,1:T(8,128)(2,1)S(1)}, bf16[256,1024]{0,1:T(8,128)(2,1)S(1)}, u32[]{:S(2)}, u32[]{:S(2)}) %collective-permute-start.29) | collective-permute-done | bytes 524320 | tf_op jit(solution)/shard_map/ppermute | solution.py:18
  377.9 10.0 %collective-permute-done.31 = bf16[256,1024]{0,1:T(8,128)(2,1)S(1)} collective-permute-done((bf16[256,1024]{0,1:T(8,128)(2,1)S(1)}, bf16[256,1024]{0,1:T(8,128)(2,1)S(1)}, u32[]{:S(2)}, u32[]{:S(2)}) %collective-permute-start.31) | collective-permute-done | bytes 524320 | tf_op jit(solution)/shard_map/ppermute | solution.py:18
  388.0 4.0 multiply_reduce_fusion
  391.9 11.5 %multiply_reduce_fusion.6 = (f32[256]{0:T(256)S(1)}, f32[256,8448]{0,1:T(8,128)S(1)}) fusion(f32[8448]{0:T(1024)S(1)} %get-tuple-element.101, s32[8448]{0:T(1024)S(1)} %get-tuple-element.102, s32[256]{0:T(256)S(1)} %dynamic_slice.6, f32[8448]{0:T(1024)S(1)} %add_rsqrt_fusion, f32[256]{0:T(256)S(1)} %add_rsqrt_fusion.1, ...), kind=kOutput, calls=%fused_computation.14 | convolution fusion | flops 4459462656 | bytes 26625280 | tf_op jit(solution)/shard_map/dot_general | solution.py:66
  403.5 3.3 copy-done
  412.2 4.5 collective-permute-start.48
  416.8 10.9 %collective-permute-start.49 = (f32[256]{0:T(256)S(1)}, f32[256]{0:T(256)S(1)}, u32[]{:S(2)}, u32[]{:S(2)}) collective-permute-start(f32[256]{0:T(256)S(1)} %get-tuple-element.81), channel_id=1, source_target_pairs={{0,2},{1,3},{2,4},{3,5},{4,6},{5,7},{6,8},{7,9},{8,10},{9,11},{10,... | collective-permute-start | bytes 3080 | tf_op jit(solution)/shard_map/ppermute | solution.py:18
  427.7 3.7 collective-permute-start.50
  431.4 3.7 collective-permute-start.51
  435.1 3.5 collective-permute-start.52
  438.7 3.6 collective-permute-start.53
  442.3 6.9 collective-permute-start.54
  486.0 4.3 collective-permute-done.45
  490.4 11.4 %collective-permute-start.64 = (f32[256]{0:T(256)S(1)}, f32[256]{0:T(256)S(1)}, u32[]{:S(2)}, u32[]{:S(2)}) collective-permute-start(f32[256]{0:T(256)S(1)} %add_divide_fusion.2), channel_id=1, source_target_pairs={{0,16},{1,17},{2,18},{3,19},{4,20},{5,21},{6,22},{7,23},{8,24},{9,... | collective-permute-start | bytes 3080 | tf_op jit(solution)/shard_map/ppermute | solution.py:18
  510.4 5.1 collective-permute-start.69
  524.2 3.3 collective-permute-start.75
  528.8 4.0 collective-permute-start.77
  579.1 5.7 multiply_reduce_fusion.4
  584.8 4.2 multiply_reduce_fusion.3
  591.6 4.5 collective-permute-start.112
  596.2 5.4 collective-permute-start.113
  609.1 6.2 collective-permute-start.117
  615.3 4.3 collective-permute-start.118
  655.3 6.6 collective-permute-done.97
  662.9 8.3 collective-permute-start.128
  680.8 3.3 collective-permute-start.135
  687.3 3.4 collective-permute-start.137
  696.7 3.5 collective-permute-start.141
  747.5 6.1 multiply_reduce_fusion.2
  753.6 4.2 multiply_reduce_fusion.1
  761.7 4.5 collective-permute-start.176
  766.3 5.4 collective-permute-start.177
  779.3 6.2 collective-permute-start.181
  785.5 4.3 collective-permute-start.182
  826.8 4.3 collective-permute-done.173
  831.1 11.4 %collective-permute-start.192 = (f32[256]{0:T(256)S(1)}, f32[256]{0:T(256)S(1)}, u32[]{:S(2)}, u32[]{:S(2)}) collective-permute-start(f32[256]{0:T(256)S(1)} %add_divide_fusion), channel_id=1, source_target_pairs={{0,16},{1,17},{2,18},{3,19},{4,20},{5,21},{6,22},{7,23},{8,24},{9,... | collective-permute-start | bytes 3080 | tf_op jit(solution)/shard_map/ppermute | solution.py:18
  851.2 5.1 collective-permute-start.197
  865.0 3.3 collective-permute-start.203
  869.6 4.0 collective-permute-start.205
  919.8 5.9 multiply_reduce_fusion.7
  925.7 12.8 %fusion.10 = bf16[256,1024]{1,0:T(8,128)(2,1)S(1)} fusion(bf16[8448,1024]{0,1:T(8,128)(2,1)} %copy-done.1, f32[256,8448]{0,1:T(8,128)} %copy-done, f32[256]{0:T(256)S(1)} %multiply_reduce_fusion.7, f32[8448]{0:T(1024)S(1)} %constant_dynamic-update-slice_fusion.38), kind=kOutput, calls=%fused_computation.21 | convolution fusion | flops 4435935232 | bytes 26511360 | tf_op jit(solution)/shard_map/dot_general | solution.py:100
  939.3 3.5 all-to-all-start.2
  943.4 13.4 %all-to-all-done.2 = bf16[256,4,256]{2,0,1:T(8,128)(2,1)S(1)} async-done(((bf16[256,4,256]{2,0,1:T(8,128)(2,1)}), bf16[256,4,256]{2,0,1:T(8,128)(2,1)S(1)}, u32[]{:S(2)}, u32[]{:S(2)}) %all-to-all-start.2) | async-done | bytes 524320 | tf_op jit(solution)/shard_map/all_to_all | solution.py:101
  (563 shorter events, 368.4 us)
Async XLA Ops:
  21.4 20.7 %all-to-all-start.1 = ((bf16[4,256,256]{2,1,0:T(8,128)(2,1)}), bf16[4,256,256]{2,1,0:T(8,128)(2,1)S(1)}, u32[]{:S(2)}, u32[]{:S(2)}) async-start(bf16[4,256,256]{2,1,0:T(8,128)(2,1)} %bitcast.64), calls=%async_computation.1 | async-start | bytes 1048576 | tf_op jit(solution)/shard_map/all_to_all | solution.py:30
  26.0 32.7 %collective-permute-start = (bf16[256,1024]{0,1:T(8,128)(2,1)S(1)}, bf16[256,1024]{0,1:T(8,128)(2,1)}, u32[]{:S(2)}, u32[]{:S(2)}) collective-permute-start(bf16[256,1024]{0,1:T(8,128)(2,1)S(1)} %bitcast.28), channel_id=1, source_target_pairs={{0,16},{1,17},{2,18},{3,19},{4,20},{5,21},{6,22},{7,23},{8,24},{9,... | collective-permute-start | bytes 1572872 | tf_op jit(solution)/shard_map/ppermute | solution.py:18
  30.2 38.1 %collective-permute-start.1 = (bf16[256,1024]{0,1:T(8,128)(2,1)S(1)}, bf16[256,1024]{0,1:T(8,128)(2,1)S(1)}, u32[]{:S(2)}, u32[]{:S(2)}) collective-permute-start(bf16[256,1024]{0,1:T(8,128)(2,1)S(1)} %bitcast.29), channel_id=1, source_target_pairs={{0,15},{1,16},{2,17},{3,18},{4,19},{5,20},{6,21},{7,22},{8,23},{9,... | collective-permute-start | bytes 1572872 | tf_op jit(solution)/shard_map/ppermute | solution.py:18
  36.2 46.0 %collective-permute-start.2 = (bf16[256,1024]{0,1:T(8,128)(2,1)S(1)}, bf16[256,1024]{0,1:T(8,128)(2,1)}, u32[]{:S(2)}, u32[]{:S(2)}) collective-permute-start(bf16[256,1024]{0,1:T(8,128)(2,1)S(1)} %bitcast.30), channel_id=1, source_target_pairs={{0,14},{1,15},{2,16},{3,17},{4,18},{5,19},{6,20},{7,21},{8,22},{9,... | collective-permute-start | bytes 1572872 | tf_op jit(solution)/shard_map/ppermute | solution.py:18
  38.3 58.1 %collective-permute-start.3 = (bf16[256,1024]{0,1:T(8,128)(2,1)S(1)}, bf16[256,1024]{0,1:T(8,128)(2,1)S(1)}, u32[]{:S(2)}, u32[]{:S(2)}) collective-permute-start(bf16[256,1024]{0,1:T(8,128)(2,1)S(1)} %bitcast.31), channel_id=1, source_target_pairs={{0,13},{1,14},{2,15},{3,16},{4,17},{5,18},{6,19},{7,20},{8,21},{9,... | collective-permute-start | bytes 1572872 | tf_op jit(solution)/shard_map/ppermute | solution.py:18
  40.7 59.1 %collective-permute-start.4 = (bf16[256,1024]{0,1:T(8,128)(2,1)S(1)}, bf16[256,1024]{0,1:T(8,128)(2,1)S(1)}, u32[]{:S(2)}, u32[]{:S(2)}) collective-permute-start(bf16[256,1024]{0,1:T(8,128)(2,1)S(1)} %bitcast.32), channel_id=1, source_target_pairs={{0,12},{1,13},{2,14},{3,15},{4,16},{5,17},{6,18},{7,19},{8,20},{9,... | collective-permute-start | bytes 1572872 | tf_op jit(solution)/shard_map/ppermute | solution.py:18
  58.6 49.9 %collective-permute-start.5 = (bf16[256,1024]{0,1:T(8,128)(2,1)S(1)}, bf16[256,1024]{0,1:T(8,128)(2,1)S(1)}, u32[]{:S(2)}, u32[]{:S(2)}) collective-permute-start(bf16[256,1024]{0,1:T(8,128)(2,1)S(1)} %bitcast.33), channel_id=1, source_target_pairs={{0,11},{1,12},{2,13},{3,14},{4,15},{5,16},{6,17},{7,18},{8,19},{9,... | collective-permute-start | bytes 1572872 | tf_op jit(solution)/shard_map/ppermute | solution.py:18
  68.3 60.0 %collective-permute-start.6 = (bf16[256,1024]{0,1:T(8,128)(2,1)S(1)}, bf16[256,1024]{0,1:T(8,128)(2,1)S(1)}, u32[]{:S(2)}, u32[]{:S(2)}) collective-permute-start(bf16[256,1024]{0,1:T(8,128)(2,1)S(1)} %bitcast.34), channel_id=1, source_target_pairs={{0,10},{1,11},{2,12},{3,13},{4,14},{5,15},{6,16},{7,17},{8,18},{9,... | collective-permute-start | bytes 1572872 | tf_op jit(solution)/shard_map/ppermute | solution.py:18
  82.2 60.2 %collective-permute-start.7 = (bf16[256,1024]{0,1:T(8,128)(2,1)S(1)}, bf16[256,1024]{0,1:T(8,128)(2,1)S(1)}, u32[]{:S(2)}, u32[]{:S(2)}) collective-permute-start(bf16[256,1024]{0,1:T(8,128)(2,1)S(1)} %bitcast.35), channel_id=1, source_target_pairs={{0,9},{1,10},{2,11},{3,12},{4,13},{5,14},{6,15},{7,16},{8,17},{9,1... | collective-permute-start | bytes 1572872 | tf_op jit(solution)/shard_map/ppermute | solution.py:18
  96.4 47.4 %collective-permute-start.8 = (bf16[256,1024]{0,1:T(8,128)(2,1)S(1)}, bf16[256,1024]{0,1:T(8,128)(2,1)S(1)}, u32[]{:S(2)}, u32[]{:S(2)}) collective-permute-start(bf16[256,1024]{0,1:T(8,128)(2,1)S(1)} %bitcast.36), channel_id=1, source_target_pairs={{0,8},{1,9},{2,10},{3,11},{4,12},{5,13},{6,14},{7,15},{8,16},{9,17... | collective-permute-start | bytes 1572872 | tf_op jit(solution)/shard_map/ppermute | solution.py:18
  99.9 68.5 %collective-permute-start.9 = (bf16[256,1024]{0,1:T(8,128)(2,1)S(1)}, bf16[256,1024]{0,1:T(8,128)(2,1)S(1)}, u32[]{:S(2)}, u32[]{:S(2)}) collective-permute-start(bf16[256,1024]{0,1:T(8,128)(2,1)S(1)} %bitcast.37), channel_id=1, source_target_pairs={{0,7},{1,8},{2,9},{3,10},{4,11},{5,12},{6,13},{7,14},{8,15},{9,16}... | collective-permute-start | bytes 1572872 | tf_op jit(solution)/shard_map/ppermute | solution.py:18
  108.6 68.0 %collective-permute-start.10 = (bf16[256,1024]{0,1:T(8,128)(2,1)S(1)}, bf16[256,1024]{0,1:T(8,128)(2,1)S(1)}, u32[]{:S(2)}, u32[]{:S(2)}) collective-permute-start(bf16[256,1024]{0,1:T(8,128)(2,1)S(1)} %bitcast.38), channel_id=1, source_target_pairs={{0,6},{1,7},{2,8},{3,9},{4,10},{5,11},{6,12},{7,13},{8,14},{9,15},... | collective-permute-start | bytes 1572872 | tf_op jit(solution)/shard_map/ppermute | solution.py:18
  128.3 49.7 %collective-permute-start.11 = (bf16[256,1024]{0,1:T(8,128)(2,1)S(1)}, bf16[256,1024]{0,1:T(8,128)(2,1)S(1)}, u32[]{:S(2)}, u32[]{:S(2)}) collective-permute-start(bf16[256,1024]{0,1:T(8,128)(2,1)S(1)} %bitcast.39), channel_id=1, source_target_pairs={{0,5},{1,6},{2,7},{3,8},{4,9},{5,10},{6,11},{7,12},{8,13},{9,14},{... | collective-permute-start | bytes 1572872 | tf_op jit(solution)/shard_map/ppermute | solution.py:18
  142.4 36.9 %collective-permute-start.12 = (bf16[256,1024]{0,1:T(8,128)(2,1)S(1)}, bf16[256,1024]{0,1:T(8,128)(2,1)S(1)}, u32[]{:S(2)}, u32[]{:S(2)}) collective-permute-start(bf16[256,1024]{0,1:T(8,128)(2,1)S(1)} %bitcast.40), channel_id=1, source_target_pairs={{0,4},{1,5},{2,6},{3,7},{4,8},{5,9},{6,10},{7,11},{8,12},{9,13},{1... | collective-permute-start | bytes 1572872 | tf_op jit(solution)/shard_map/ppermute | solution.py:18
  143.8 36.8 %collective-permute-start.13 = (bf16[256,1024]{0,1:T(8,128)(2,1)S(1)}, bf16[256,1024]{0,1:T(8,128)(2,1)S(1)}, u32[]{:S(2)}, u32[]{:S(2)}) collective-permute-start(bf16[256,1024]{0,1:T(8,128)(2,1)S(1)} %bitcast.41), channel_id=1, source_target_pairs={{0,3},{1,4},{2,5},{3,6},{4,7},{5,8},{6,9},{7,10},{8,11},{9,12},{10... | collective-permute-start | bytes 1572872 | tf_op jit(solution)/shard_map/ppermute | solution.py:18
  168.4 23.5 %collective-permute-start.14 = (bf16[256,1024]{0,1:T(8,128)(2,1)S(1)}, bf16[256,1024]{0,1:T(8,128)(2,1)S(1)}, u32[]{:S(2)}, u32[]{:S(2)}) collective-permute-start(bf16[256,1024]{0,1:T(8,128)(2,1)S(1)} %bitcast.42), channel_id=1, source_target_pairs={{0,2},{1,3},{2,4},{3,5},{4,6},{5,7},{6,8},{7,9},{8,10},{9,11},{10,... | collective-permute-start | bytes 1572872 | tf_op jit(solution)/shard_map/ppermute | solution.py:18
  176.6 26.5 %collective-permute-start.15 = (bf16[256,1024]{0,1:T(8,128)(2,1)S(1)}, bf16[256,1024]{0,1:T(8,128)(2,1)S(1)}, u32[]{:S(2)}, u32[]{:S(2)}) collective-permute-start(bf16[256,1024]{0,1:T(8,128)(2,1)S(1)} %bitcast.43), channel_id=1, source_target_pairs={{0,1},{1,2},{2,3},{3,4},{4,5},{5,6},{6,7},{7,8},{8,9},{9,10},{10,1... | collective-permute-start | bytes 1572872 | tf_op jit(solution)/shard_map/ppermute | solution.py:18
  178.0 48.9 %collective-permute-start.16 = (bf16[256,1024]{0,1:T(8,128)(2,1)S(1)}, bf16[256,1024]{0,1:T(8,128)(2,1)S(1)}, u32[]{:S(2)}, u32[]{:S(2)}) collective-permute-start(bf16[256,1024]{0,1:T(8,128)(2,1)S(1)} %bitcast.44), channel_id=1, source_target_pairs={{1,0},{2,1},{3,2},{4,3},{5,4},{6,5},{7,6},{8,7},{9,8},{10,9},{11,1... | collective-permute-start | bytes 1572872 | tf_op jit(solution)/shard_map/ppermute | solution.py:18
  179.3 102.6 %collective-permute-start.17 = (bf16[256,1024]{0,1:T(8,128)(2,1)S(1)}, bf16[256,1024]{0,1:T(8,128)(2,1)S(1)}, u32[]{:S(2)}, u32[]{:S(2)}) collective-permute-start(bf16[256,1024]{0,1:T(8,128)(2,1)S(1)} %bitcast.45), channel_id=1, source_target_pairs={{2,0},{3,1},{4,2},{5,3},{6,4},{7,5},{8,6},{9,7},{10,8},{11,9},{12,... | collective-permute-start | bytes 1572872 | tf_op jit(solution)/shard_map/ppermute | solution.py:18
  180.7 102.5 %collective-permute-start.18 = (bf16[256,1024]{0,1:T(8,128)(2,1)S(1)}, bf16[256,1024]{0,1:T(8,128)(2,1)S(1)}, u32[]{:S(2)}, u32[]{:S(2)}) collective-permute-start(bf16[256,1024]{0,1:T(8,128)(2,1)S(1)} %bitcast.46), channel_id=1, source_target_pairs={{3,0},{4,1},{5,2},{6,3},{7,4},{8,5},{9,6},{10,7},{11,8},{12,9},{13... | collective-permute-start | bytes 1572872 | tf_op jit(solution)/shard_map/ppermute | solution.py:18
  191.9 92.7 %collective-permute-start.19 = (bf16[256,1024]{0,1:T(8,128)(2,1)S(1)}, bf16[256,1024]{0,1:T(8,128)(2,1)S(1)}, u32[]{:S(2)}, u32[]{:S(2)}) collective-permute-start(bf16[256,1024]{0,1:T(8,128)(2,1)S(1)} %bitcast.47), channel_id=1, source_target_pairs={{4,0},{5,1},{6,2},{7,3},{8,4},{9,5},{10,6},{11,7},{12,8},{13,9},{1... | collective-permute-start | bytes 1572872 | tf_op jit(solution)/shard_map/ppermute | solution.py:18
  203.1 82.9 %collective-permute-start.20 = (bf16[256,1024]{0,1:T(8,128)(2,1)S(1)}, bf16[256,1024]{0,1:T(8,128)(2,1)S(1)}, u32[]{:S(2)}, u32[]{:S(2)}) collective-permute-start(bf16[256,1024]{0,1:T(8,128)(2,1)S(1)} %bitcast.48), channel_id=1, source_target_pairs={{5,0},{6,1},{7,2},{8,3},{9,4},{10,5},{11,6},{12,7},{13,8},{14,9},{... | collective-permute-start | bytes 1572872 | tf_op jit(solution)/shard_map/ppermute | solution.py:18
  226.9 70.8 %collective-permute-start.21 = (bf16[256,1024]{0,1:T(8,128)(2,1)S(1)}, bf16[256,1024]{0,1:T(8,128)(2,1)S(1)}, u32[]{:S(2)}, u32[]{:S(2)}) collective-permute-start(bf16[256,1024]{0,1:T(8,128)(2,1)S(1)} %bitcast.50), channel_id=1, source_target_pairs={{6,0},{7,1},{8,2},{9,3},{10,4},{11,5},{12,6},{13,7},{14,8},{15,9},... | collective-permute-start | bytes 1572872 | tf_op jit(solution)/shard_map/ppermute | solution.py:18
  281.9 17.1 %collective-permute-start.22 = (bf16[256,1024]{0,1:T(8,128)(2,1)S(1)}, bf16[256,1024]{0,1:T(8,128)(2,1)S(1)}, u32[]{:S(2)}, u32[]{:S(2)}) collective-permute-start(bf16[256,1024]{0,1:T(8,128)(2,1)S(1)} %bitcast.51), channel_id=1, source_target_pairs={{7,0},{8,1},{9,2},{10,3},{11,4},{12,5},{13,6},{14,7},{15,8},{16,9}... | collective-permute-start | bytes 1572872 | tf_op jit(solution)/shard_map/ppermute | solution.py:18
  283.2 40.4 %collective-permute-start.23 = (bf16[256,1024]{0,1:T(8,128)(2,1)S(1)}, bf16[256,1024]{0,1:T(8,128)(2,1)S(1)}, u32[]{:S(2)}, u32[]{:S(2)}) collective-permute-start(bf16[256,1024]{0,1:T(8,128)(2,1)S(1)} %bitcast.52), channel_id=1, source_target_pairs={{8,0},{9,1},{10,2},{11,3},{12,4},{13,5},{14,6},{15,7},{16,8},{17,9... | collective-permute-start | bytes 1572872 | tf_op jit(solution)/shard_map/ppermute | solution.py:18
  284.6 40.4 %collective-permute-start.24 = (bf16[256,1024]{0,1:T(8,128)(2,1)S(1)}, bf16[256,1024]{0,1:T(8,128)(2,1)S(1)}, u32[]{:S(2)}, u32[]{:S(2)}) collective-permute-start(bf16[256,1024]{0,1:T(8,128)(2,1)S(1)} %bitcast.53), channel_id=1, source_target_pairs={{9,0},{10,1},{11,2},{12,3},{13,4},{14,5},{15,6},{16,7},{17,8},{18,... | collective-permute-start | bytes 1572872 | tf_op jit(solution)/shard_map/ppermute | solution.py:18
  285.9 76.0 %collective-permute-start.25 = (bf16[256,1024]{0,1:T(8,128)(2,1)S(1)}, bf16[256,1024]{0,1:T(8,128)(2,1)S(1)}, u32[]{:S(2)}, u32[]{:S(2)}) collective-permute-start(bf16[256,1024]{0,1:T(8,128)(2,1)S(1)} %bitcast.54), channel_id=1, source_target_pairs={{10,0},{11,1},{12,2},{13,3},{14,4},{15,5},{16,6},{17,7},{18,8},{19... | collective-permute-start | bytes 1572872 | tf_op jit(solution)/shard_map/ppermute | solution.py:18
  297.7 65.6 %collective-permute-start.26 = (bf16[256,1024]{0,1:T(8,128)(2,1)S(1)}, bf16[256,1024]{0,1:T(8,128)(2,1)S(1)}, u32[]{:S(2)}, u32[]{:S(2)}) collective-permute-start(bf16[256,1024]{0,1:T(8,128)(2,1)S(1)} %bitcast.55), channel_id=1, source_target_pairs={{11,0},{12,1},{13,2},{14,3},{15,4},{16,5},{17,6},{18,7},{19,8},{20... | collective-permute-start | bytes 1572872 | tf_op jit(solution)/shard_map/ppermute | solution.py:18
  299.0 65.6 %collective-permute-start.27 = (bf16[256,1024]{0,1:T(8,128)(2,1)S(1)}, bf16[256,1024]{0,1:T(8,128)(2,1)S(1)}, u32[]{:S(2)}, u32[]{:S(2)}) collective-permute-start(bf16[256,1024]{0,1:T(8,128)(2,1)S(1)} %bitcast.56), channel_id=1, source_target_pairs={{12,0},{13,1},{14,2},{15,3},{16,4},{17,5},{18,6},{19,7},{20,8},{21... | collective-permute-start | bytes 1572872 | tf_op jit(solution)/shard_map/ppermute | solution.py:18
  323.7 41.0 %collective-permute-start.28 = (bf16[256,1024]{0,1:T(8,128)(2,1)S(1)}, bf16[256,1024]{0,1:T(8,128)(2,1)S(1)}, u32[]{:S(2)}, u32[]{:S(2)}) collective-permute-start(bf16[256,1024]{0,1:T(8,128)(2,1)S(1)} %bitcast.57), channel_id=1, source_target_pairs={{13,0},{14,1},{15,2},{16,3},{17,4},{18,5},{19,6},{20,7},{21,8},{22... | collective-permute-start | bytes 1572872 | tf_op jit(solution)/shard_map/ppermute | solution.py:18
  325.0 52.7 %collective-permute-start.29 = (bf16[256,1024]{0,1:T(8,128)(2,1)S(1)}, bf16[256,1024]{0,1:T(8,128)(2,1)S(1)}, u32[]{:S(2)}, u32[]{:S(2)}) collective-permute-start(bf16[256,1024]{0,1:T(8,128)(2,1)S(1)} %bitcast.58), channel_id=1, source_target_pairs={{14,0},{15,1},{16,2},{17,3},{18,4},{19,5},{20,6},{21,7},{22,8},{23... | collective-permute-start | bytes 1572872 | tf_op jit(solution)/shard_map/ppermute | solution.py:18
  362.0 15.8 %collective-permute-start.30 = (bf16[256,1024]{0,1:T(8,128)(2,1)S(1)}, bf16[256,1024]{0,1:T(8,128)(2,1)S(1)}, u32[]{:S(2)}, u32[]{:S(2)}) collective-permute-start(bf16[256,1024]{0,1:T(8,128)(2,1)S(1)} %bitcast.59), channel_id=1, source_target_pairs={{15,0},{16,1},{17,2},{18,3},{19,4},{20,5},{21,6},{22,7},{23,8},{24... | collective-permute-start | bytes 1572872 | tf_op jit(solution)/shard_map/ppermute | solution.py:18
  363.3 24.6 %collective-permute-start.31 = (bf16[256,1024]{0,1:T(8,128)(2,1)S(1)}, bf16[256,1024]{0,1:T(8,128)(2,1)S(1)}, u32[]{:S(2)}, u32[]{:S(2)}) collective-permute-start(bf16[256,1024]{0,1:T(8,128)(2,1)S(1)} %bitcast.60), channel_id=1, source_target_pairs={{16,0},{17,1},{18,2},{19,3},{20,4},{21,5},{22,6},{23,7},{24,8},{25... | collective-permute-start | bytes 1572872 | tf_op jit(solution)/shard_map/ppermute | solution.py:18
  408.3 19.3 %collective-permute-start.32 = (f32[256]{0:T(256)S(1)}, f32[256]{0:T(256)S(1)}, u32[]{:S(2)}, u32[]{:S(2)}) collective-permute-start(f32[256]{0:T(256)S(1)} %get-tuple-element.66), channel_id=1, source_target_pairs={{16,0},{17,1},{18,2},{19,3},{20,4},{21,5},{22,6},{23,7},{24,8},{25... | collective-permute-start | bytes 3080 | tf_op jit(solution)/shard_map/ppermute | solution.py:18
  409.6 21.8 %collective-permute-start.46 = (f32[256]{0:T(256)S(1)}, f32[256]{0:T(256)S(1)}, u32[]{:S(2)}, u32[]{:S(2)}) collective-permute-start(f32[256]{0:T(256)S(1)} %get-tuple-element.84), channel_id=1, source_target_pairs={{2,0},{3,1},{4,2},{5,3},{6,4},{7,5},{8,6},{9,7},{10,8},{11,9},{12,... | collective-permute-start | bytes 3080 | tf_op jit(solution)/shard_map/ppermute | solution.py:18
  410.9 24.2 %collective-permute-start.47 = (f32[256]{0:T(256)S(1)}, f32[256]{0:T(256)S(1)}, u32[]{:S(2)}, u32[]{:S(2)}) collective-permute-start(f32[256]{0:T(256)S(1)} %get-tuple-element.83), channel_id=1, source_target_pairs={{1,0},{2,1},{3,2},{4,3},{5,4},{6,5},{7,6},{8,7},{9,8},{10,9},{11,1... | collective-permute-start | bytes 3080 | tf_op jit(solution)/shard_map/ppermute | solution.py:18
  412.2 26.4 %collective-permute-start.48 = (f32[256]{0:T(256)S(1)}, f32[256]{0:T(256)S(1)}, u32[]{:S(2)}, u32[]{:S(2)}) collective-permute-start(f32[256]{0:T(256)S(1)} %get-tuple-element.82), channel_id=1, source_target_pairs={{0,1},{1,2},{2,3},{3,4},{4,5},{5,6},{6,7},{7,8},{8,9},{9,10},{10,1... | collective-permute-start | bytes 3080 | tf_op jit(solution)/shard_map/ppermute | solution.py:18
  416.8 25.5 %collective-permute-start.49 = (f32[256]{0:T(256)S(1)}, f32[256]{0:T(256)S(1)}, u32[]{:S(2)}, u32[]{:S(2)}) collective-permute-start(f32[256]{0:T(256)S(1)} %get-tuple-element.81), channel_id=1, source_target_pairs={{0,2},{1,3},{2,4},{3,5},{4,6},{5,7},{6,8},{7,9},{8,10},{9,11},{10,... | collective-permute-start | bytes 3080 | tf_op jit(solution)/shard_map/ppermute | solution.py:18
  427.7 21.5 %collective-permute-start.50 = (f32[256]{0:T(256)S(1)}, f32[256]{0:T(256)S(1)}, u32[]{:S(2)}, u32[]{:S(2)}) collective-permute-start(f32[256]{0:T(256)S(1)} %get-tuple-element.80), channel_id=1, source_target_pairs={{0,3},{1,4},{2,5},{3,6},{4,7},{5,8},{6,9},{7,10},{8,11},{9,12},{10... | collective-permute-start | bytes 3080 | tf_op jit(solution)/shard_map/ppermute | solution.py:18
  431.4 19.9 %collective-permute-start.51 = (f32[256]{0:T(256)S(1)}, f32[256]{0:T(256)S(1)}, u32[]{:S(2)}, u32[]{:S(2)}) collective-permute-start(f32[256]{0:T(256)S(1)} %get-tuple-element.79), channel_id=1, source_target_pairs={{0,4},{1,5},{2,6},{3,7},{4,8},{5,9},{6,10},{7,11},{8,12},{9,13},{1... | collective-permute-start | bytes 3080 | tf_op jit(solution)/shard_map/ppermute | solution.py:18
  435.1 18.1 %collective-permute-start.52 = (f32[256]{0:T(256)S(1)}, f32[256]{0:T(256)S(1)}, u32[]{:S(2)}, u32[]{:S(2)}) collective-permute-start(f32[256]{0:T(256)S(1)} %get-tuple-element.78), channel_id=1, source_target_pairs={{0,5},{1,6},{2,7},{3,8},{4,9},{5,10},{6,11},{7,12},{8,13},{9,14},{... | collective-permute-start | bytes 3080 | tf_op jit(solution)/shard_map/ppermute | solution.py:18
  438.7 16.5 %collective-permute-start.53 = (f32[256]{0:T(256)S(1)}, f32[256]{0:T(256)S(1)}, u32[]{:S(2)}, u32[]{:S(2)}) collective-permute-start(f32[256]{0:T(256)S(1)} %get-tuple-element.77), channel_id=1, source_target_pairs={{0,6},{1,7},{2,8},{3,9},{4,10},{5,11},{6,12},{7,13},{8,14},{9,15},... | collective-permute-start | bytes 3080 | tf_op jit(solution)/shard_map/ppermute | solution.py:18
  442.3 14.8 %collective-permute-start.54 = (f32[256]{0:T(256)S(1)}, f32[256]{0:T(256)S(1)}, u32[]{:S(2)}, u32[]{:S(2)}) collective-permute-start(f32[256]{0:T(256)S(1)} %get-tuple-element.76), channel_id=1, source_target_pairs={{0,7},{1,8},{2,9},{3,10},{4,11},{5,12},{6,13},{7,14},{8,15},{9,16}... | collective-permute-start | bytes 3080 | tf_op jit(solution)/shard_map/ppermute | solution.py:18
  490.4 20.1 %collective-permute-start.64 = (f32[256]{0:T(256)S(1)}, f32[256]{0:T(256)S(1)}, u32[]{:S(2)}, u32[]{:S(2)}) collective-permute-start(f32[256]{0:T(256)S(1)} %add_divide_fusion.2), channel_id=1, source_target_pairs={{0,16},{1,17},{2,18},{3,19},{4,20},{5,21},{6,22},{7,23},{8,24},{9,... | collective-permute-start | bytes 3080 | tf_op jit(solution)/shard_map/ppermute | solution.py:18
  589.0 15.7 %collective-permute-start.110 = (f32[256]{0:T(256)S(1)}, f32[256]{0:T(256)S(1)}, u32[]{:S(2)}, u32[]{:S(2)}) collective-permute-start(f32[256]{0:T(256)S(1)} %get-tuple-element.52), channel_id=1, source_target_pairs={{2,0},{3,1},{4,2},{5,3},{6,4},{7,5},{8,6},{9,7},{10,8},{11,9},{12,... | collective-permute-start | bytes 3080 | tf_op jit(solution)/shard_map/ppermute | solution.py:18
  590.3 16.1 %collective-permute-start.111 = (f32[256]{0:T(256)S(1)}, f32[256]{0:T(256)S(1)}, u32[]{:S(2)}, u32[]{:S(2)}) collective-permute-start(f32[256]{0:T(256)S(1)} %get-tuple-element.51), channel_id=1, source_target_pairs={{1,0},{2,1},{3,2},{4,3},{5,4},{6,5},{7,6},{8,7},{9,8},{10,9},{11,1... | collective-permute-start | bytes 3080 | tf_op jit(solution)/shard_map/ppermute | solution.py:18
  591.6 17.5 %collective-permute-start.112 = (f32[256]{0:T(256)S(1)}, f32[256]{0:T(256)S(1)}, u32[]{:S(2)}, u32[]{:S(2)}) collective-permute-start(f32[256]{0:T(256)S(1)} %get-tuple-element.50), channel_id=1, source_target_pairs={{0,1},{1,2},{2,3},{3,4},{4,5},{5,6},{6,7},{7,8},{8,9},{9,10},{10,1... | collective-permute-start | bytes 3080 | tf_op jit(solution)/shard_map/ppermute | solution.py:18
  596.2 19.2 %collective-permute-start.113 = (f32[256]{0:T(256)S(1)}, f32[256]{0:T(256)S(1)}, u32[]{:S(2)}, u32[]{:S(2)}) collective-permute-start(f32[256]{0:T(256)S(1)} %get-tuple-element.49), channel_id=1, source_target_pairs={{0,2},{1,3},{2,4},{3,5},{4,6},{5,7},{6,8},{7,9},{8,10},{9,11},{10,... | collective-permute-start | bytes 3080 | tf_op jit(solution)/shard_map/ppermute | solution.py:18
  601.6 18.0 %collective-permute-start.114 = (f32[256]{0:T(256)S(1)}, f32[256]{0:T(256)S(1)}, u32[]{:S(2)}, u32[]{:S(2)}) collective-permute-start(f32[256]{0:T(256)S(1)} %get-tuple-element.48), channel_id=1, source_target_pairs={{0,3},{1,4},{2,5},{3,6},{4,7},{5,8},{6,9},{7,10},{8,11},{9,12},{10... | collective-permute-start | bytes 3080 | tf_op jit(solution)/shard_map/ppermute | solution.py:18
  604.7 16.2 %collective-permute-start.115 = (f32[256]{0:T(256)S(1)}, f32[256]{0:T(256)S(1)}, u32[]{:S(2)}, u32[]{:S(2)}) collective-permute-start(f32[256]{0:T(256)S(1)} %get-tuple-element.47), channel_id=1, source_target_pairs={{0,4},{1,5},{2,6},{3,7},{4,8},{5,9},{6,10},{7,11},{8,12},{9,13},{1... | collective-permute-start | bytes 3080 | tf_op jit(solution)/shard_map/ppermute | solution.py:18
  606.4 15.8 %collective-permute-start.116 = (f32[256]{0:T(256)S(1)}, f32[256]{0:T(256)S(1)}, u32[]{:S(2)}, u32[]{:S(2)}) collective-permute-start(f32[256]{0:T(256)S(1)} %get-tuple-element.46), channel_id=1, source_target_pairs={{0,5},{1,6},{2,7},{3,8},{4,9},{5,10},{6,11},{7,12},{8,13},{9,14},{... | collective-permute-start | bytes 3080 | tf_op jit(solution)/shard_map/ppermute | solution.py:18
  609.1 14.4 %collective-permute-start.117 = (f32[256]{0:T(256)S(1)}, f32[256]{0:T(256)S(1)}, u32[]{:S(2)}, u32[]{:S(2)}) collective-permute-start(f32[256]{0:T(256)S(1)} %get-tuple-element.45), channel_id=1, source_target_pairs={{0,6},{1,7},{2,8},{3,9},{4,10},{5,11},{6,12},{7,13},{8,14},{9,15},... | collective-permute-start | bytes 3080 | tf_op jit(solution)/shard_map/ppermute | solution.py:18
  662.9 15.0 %collective-permute-start.128 = (f32[256]{0:T(256)S(1)}, f32[256]{0:T(256)S(1)}, u32[]{:S(2)}, u32[]{:S(2)}) collective-permute-start(f32[256]{0:T(256)S(1)} %add_divide_fusion.1), channel_id=1, source_target_pairs={{0,16},{1,17},{2,18},{3,19},{4,20},{5,21},{6,22},{7,23},{8,24},{9,... | collective-permute-start | bytes 3080 | tf_op jit(solution)/shard_map/ppermute | solution.py:18
  757.8 13.9 %collective-permute-start.160 = (f32[256]{0:T(256)S(1)}, f32[256]{0:T(256)S(1)}, u32[]{:S(2)}, u32[]{:S(2)}) collective-permute-start(f32[256]{0:T(256)S(1)} %get-tuple-element.2), channel_id=1, source_target_pairs={{16,0},{17,1},{18,2},{19,3},{20,4},{21,5},{22,6},{23,7},{24,8},{25... | collective-permute-start | bytes 3080 | tf_op jit(solution)/shard_map/ppermute | solution.py:18
  759.1 15.7 %collective-permute-start.174 = (f32[256]{0:T(256)S(1)}, f32[256]{0:T(256)S(1)}, u32[]{:S(2)}, u32[]{:S(2)}) collective-permute-start(f32[256]{0:T(256)S(1)} %get-tuple-element.20), channel_id=1, source_target_pairs={{2,0},{3,1},{4,2},{5,3},{6,4},{7,5},{8,6},{9,7},{10,8},{11,9},{12,... | collective-permute-start | bytes 3080 | tf_op jit(solution)/shard_map/ppermute | solution.py:18
  760.4 16.1 %collective-permute-start.175 = (f32[256]{0:T(256)S(1)}, f32[256]{0:T(256)S(1)}, u32[]{:S(2)}, u32[]{:S(2)}) collective-permute-start(f32[256]{0:T(256)S(1)} %get-tuple-element.19), channel_id=1, source_target_pairs={{1,0},{2,1},{3,2},{4,3},{5,4},{6,5},{7,6},{8,7},{9,8},{10,9},{11,1... | collective-permute-start | bytes 3080 | tf_op jit(solution)/shard_map/ppermute | solution.py:18
  761.7 17.5 %collective-permute-start.176 = (f32[256]{0:T(256)S(1)}, f32[256]{0:T(256)S(1)}, u32[]{:S(2)}, u32[]{:S(2)}) collective-permute-start(f32[256]{0:T(256)S(1)} %get-tuple-element.18), channel_id=1, source_target_pairs={{0,1},{1,2},{2,3},{3,4},{4,5},{5,6},{6,7},{7,8},{8,9},{9,10},{10,1... | collective-permute-start | bytes 3080 | tf_op jit(solution)/shard_map/ppermute | solution.py:18
  766.3 19.2 %collective-permute-start.177 = (f32[256]{0:T(256)S(1)}, f32[256]{0:T(256)S(1)}, u32[]{:S(2)}, u32[]{:S(2)}) collective-permute-start(f32[256]{0:T(256)S(1)} %get-tuple-element.17), channel_id=1, source_target_pairs={{0,2},{1,3},{2,4},{3,5},{4,6},{5,7},{6,8},{7,9},{8,10},{9,11},{10,... | collective-permute-start | bytes 3080 | tf_op jit(solution)/shard_map/ppermute | solution.py:18
  771.7 18.0 %collective-permute-start.178 = (f32[256]{0:T(256)S(1)}, f32[256]{0:T(256)S(1)}, u32[]{:S(2)}, u32[]{:S(2)}) collective-permute-start(f32[256]{0:T(256)S(1)} %get-tuple-element.16), channel_id=1, source_target_pairs={{0,3},{1,4},{2,5},{3,6},{4,7},{5,8},{6,9},{7,10},{8,11},{9,12},{10... | collective-permute-start | bytes 3080 | tf_op jit(solution)/shard_map/ppermute | solution.py:18
  774.8 17.2 %collective-permute-start.179 = (f32[256]{0:T(256)S(1)}, f32[256]{0:T(256)S(1)}, u32[]{:S(2)}, u32[]{:S(2)}) collective-permute-start(f32[256]{0:T(256)S(1)} %get-tuple-element.15), channel_id=1, source_target_pairs={{0,4},{1,5},{2,6},{3,7},{4,8},{5,9},{6,10},{7,11},{8,12},{9,13},{1... | collective-permute-start | bytes 3080 | tf_op jit(solution)/shard_map/ppermute | solution.py:18
  776.5 17.4 %collective-permute-start.180 = (f32[256]{0:T(256)S(1)}, f32[256]{0:T(256)S(1)}, u32[]{:S(2)}, u32[]{:S(2)}) collective-permute-start(f32[256]{0:T(256)S(1)} %get-tuple-element.14), channel_id=1, source_target_pairs={{0,5},{1,6},{2,7},{3,8},{4,9},{5,10},{6,11},{7,12},{8,13},{9,14},{... | collective-permute-start | bytes 3080 | tf_op jit(solution)/shard_map/ppermute | solution.py:18
  779.3 16.7 %collective-permute-start.181 = (f32[256]{0:T(256)S(1)}, f32[256]{0:T(256)S(1)}, u32[]{:S(2)}, u32[]{:S(2)}) collective-permute-start(f32[256]{0:T(256)S(1)} %get-tuple-element.13), channel_id=1, source_target_pairs={{0,6},{1,7},{2,8},{3,9},{4,10},{5,11},{6,12},{7,13},{8,14},{9,15},... | collective-permute-start | bytes 3080 | tf_op jit(solution)/shard_map/ppermute | solution.py:18
  831.1 20.1 %collective-permute-start.192 = (f32[256]{0:T(256)S(1)}, f32[256]{0:T(256)S(1)}, u32[]{:S(2)}, u32[]{:S(2)}) collective-permute-start(f32[256]{0:T(256)S(1)} %add_divide_fusion), channel_id=1, source_target_pairs={{0,16},{1,17},{2,18},{3,19},{4,20},{5,21},{6,22},{7,23},{8,24},{9,... | collective-permute-start | bytes 3080 | tf_op jit(solution)/shard_map/ppermute | solution.py:18
  939.3 17.4 %all-to-all-start.2 = ((bf16[256,4,256]{2,0,1:T(8,128)(2,1)}), bf16[256,4,256]{2,0,1:T(8,128)(2,1)S(1)}, u32[]{:S(2)}, u32[]{:S(2)}) async-start(bf16[256,4,256]{2,0,1:T(8,128)(2,1)} %bitcast.26), calls=%async_computation.2 | async-start | bytes 1048576 | tf_op jit(solution)/shard_map/all_to_all | solution.py:101
  (164 other events, 1572.3 us)
where the time goes:
time: 969 us; the launch traced here: 958 us
  starting transfers between devices  557 us (57%)
  waiting for transfers between devices  307 us (32%)
  other arithmetic  33.3 us (3%)
  matrix products  24.3 us (3%)
  blocking collectives  20.8 us (2%)
  local copies, waits for them, and re-layouts  10.9 us (1%)
    ppermute x224, starting transfers between devices, shifted_2(): return lax.ppermute(block, axis, route)  550 us
    ppermute x224, waiting for transfers between devices, shifted_2(): return lax.ppermute(block, axis, route)  293 us
    all_to_all x1, blocking collectives, per_device(): lax.all_to_all(target, 'emb', split_axis=0, concat_axis=1, tiled=True)  20.8 us
  transfers between devices with their start and end apart: 226, of which 66 were waited for; matrix products, arithmetic and copies ran while one was open for 1% of the time, Pallas kernels for 0%

commit v1 on v0

--- a/solution.py
+++ b/solution.py
@@ -1,6 +1,10 @@
+import functools
+
 import jax
 import jax.numpy as jnp
 from jax import lax
+from jax.experimental import pallas as pl
+from jax.experimental.pallas import tpu as pltpu
 from jax.sharding import PartitionSpec as P
 
 BAND = 2048
@@ -102,9 +106,375 @@
     return (projected, row_mass)
 
 
+F32 = jnp.float32
+BF16 = jnp.bfloat16
+MESH = pl.DeviceIdType.MESH
+
+
+def flip(value, mask):
+    for bit in (1, 2, 4):
+        if mask & bit:
+            value = value + bit * (1 - 2 * ((value // bit) % 2))
+    return value
+
+
+def fused_kernel(
+    src_in, tgt_in, offs_in, sdoc, tdoc, out, mass,
+    src_all, tgt_all, offs, kmat, wmat, sscale, tscale, rowacc, rowbuf, invcol, invrow, scal, colpart,
+    colbuf, piece, pieces_in, z_ssem, z_rsem, t_ssem, t_rsem, row_ssem, row_rsem, col_ssem, col_rsem,
+    p_ssem, p_rsem,
+):
+    n_seq, n_emb = lax.axis_size("seq"), lax.axis_size("emb")
+    s, e = lax.axis_index("seq"), lax.axis_index("emb")
+    eh, el = e // 2, e % 2
+    block, feats = src_in.shape
+    rows = src_all.shape[0]
+    held = block // 2
+    half = held // 2
+
+    def remote(src, dst, ssem, rsem, seq, emb):
+        return pltpu.make_async_remote_copy(
+            src_ref=src, dst_ref=dst, send_sem=ssem, recv_sem=rsem,
+            device_id=(seq, emb), device_id_type=MESH,
+        )
+
+    barrier = pltpu.get_barrier_semaphore()
+    for j in range(1, n_emb):
+        pl.semaphore_signal(barrier, inc=1, device_id=(s, flip(e, j)), device_id_type=MESH)
+    for k in range(1, n_seq):
+        pl.semaphore_signal(barrier, inc=1, device_id=(flip(s, k), e), device_id_type=MESH)
+        pl.semaphore_signal(barrier, inc=1, device_id=(flip(s, k), flip(e, 2)), device_id_type=MESH)
+    pl.semaphore_wait(barrier, n_emb - 1 + 2 * (n_seq - 1))
+
+    def cols(f):
+        return pl.ds(pl.multiple_of(f * feats, feats), feats)
+
+    def region(slot, j, start=0, count=held):
+        return tgt_all.at[pl.ds(pl.multiple_of(slot * held + start, half), count), cols(flip(e, j))]
+
+    sent = []
+
+    def start(copy):
+        copy.start()
+        sent.append(copy)
+
+    mine_t = pl.ds(pl.multiple_of(s * held, held), held)
+    for j in range(1, n_emb):
+        peer = flip(e, j)
+        start(remote(
+            tgt_in.at[pl.ds(pl.multiple_of((peer % 2) * held, held), held), :],
+            tgt_all.at[mine_t, cols(e)], z_ssem.at[0, j], z_rsem.at[0, j], s, peer,
+        ))
+    start(remote(offs_in, offs.at[el], z_ssem.at[2, 0], z_rsem.at[2, 0], s, flip(e, 1)))
+    for j in range(1, n_emb):
+        peer = flip(e, j)
+        start(remote(
+            src_in.at[pl.ds(pl.multiple_of((peer // 2) * rows, rows), rows), :],
+            src_all.at[:, cols(e)], z_ssem.at[1, j], z_rsem.at[1, j], s, peer,
+        ))
+    tgt_all[mine_t, cols(e)] = tgt_in[pl.ds(pl.multiple_of(el * held, held), held), :]
+    src_all[:, cols(e)] = src_in[pl.ds(pl.multiple_of(eh * rows, rows), rows), :]
+    offs[el] = offs_in[...]
+
+    count = [0]
+
+    def send(slot, j, k, to, begin=0, length=held, part=0):
+        at = region(slot, j, begin, length)
+        start(remote(at, at, t_ssem.at[count[0]], t_rsem.at[k, j, part], flip(s, to), e))
+        count[0] += 1
+
+    def arrived(k, j, begin=0, length=held, part=0):
+        at = region(flip(s, k), j, begin, length)
+        remote(at, at, t_ssem.at[0], t_rsem.at[k, j, part], s, e).wait_recv()
+
+    def first(j):
+        if j:
+            at = region(s, j)
+            remote(at, at, z_ssem.at[0, 0], z_rsem.at[0, j], s, e).wait_recv()
+        send(s, j, 2, 2)
+        send(s, j, 4, 4)
+        send(s, j, 1, 1)
+
+    def second(j):
+        arrived(2, j)
+        send(flip(s, 2), j, 6, 4, 0, half, 0)
+        send(flip(s, 2), j, 3, 1)
+        arrived(4, j)
+        send(flip(s, 4), j, 6, 2, half, half, 1)
+        send(flip(s, 4), j, 5, 1)
+
+    def third(j):
+        for part in range(2):
+            arrived(6, j, part * half, half, part)
+            send(flip(s, 6), j, 7, 1, part * half, half, part)
+
+    for step in range(n_emb + 2):
+        for stage, lag in ((first, 0), (second, 1), (third, 2)):
+            if 0 <= step - lag < n_emb:
+                stage(step - lag)
+
+    for j in range(1, n_emb):
+        at = src_all.at[:, cols(flip(e, j))]
+        remote(at, at, z_ssem.at[1, 0], z_rsem.at[1, j], s, e).wait_recv()
+    at = offs.at[1 - el]
+    remote(at, at, z_ssem.at[2, 0], z_rsem.at[2, 0], s, e).wait_recv()
+
+    lanes = 128
+    depth = src_all.shape[1]
+
+    @pl.loop(0, rows // 64)
+    def _(r):
+        at = pl.ds(pl.multiple_of(r * 64, 64), 64)
+        acc = jnp.zeros((64, lanes), F32)
+        for c in range(depth // lanes):
+            x = src_all[at, pl.ds(c * lanes, lanes)].astype(F32)
+            acc = acc + x * x
+        total = jnp.sum(acc, axis=1, keepdims=True)
+        sscale[at, :] = jnp.broadcast_to(lax.rsqrt(total + 1e-6), (64, lanes))
+
+    for j in range(n_emb):
+        for k in (1, 3, 5):
+            arrived(k, j)
+        for part in range(2):
+            arrived(7, j, part * half, half, part)
+
+    @pl.loop(0, n_seq)
+    def _(slot):
+        base = slot * held
+        at = pl.ds(pl.multiple_of(base, held), held)
+
+        @pl.loop(0, rows // 256)
+        def _(r):
+            rt = pl.ds(pl.multiple_of(r * 256, 256), 256)
+            kmat[rt, at] = lax.dot_general(
+                src_all[rt, :], tgt_all[at, :], (((1,), (1,)), ((), ())),
+                preferred_element_type=F32,
+            )
+
+        @pl.loop(0, held // lanes)
+        def _(c):
+            tt = pl.ds(pl.multiple_of(base + c * lanes, lanes), lanes)
+            acc = jnp.zeros((lanes, lanes), F32)
+            for d in range(depth // lanes):
+                x = tgt_all[tt, pl.ds(d * lanes, lanes)].astype(F32)
+                acc = acc + x * x
+            total = jnp.sum(jnp.transpose(acc), axis=0, keepdims=True)
+            tscale[slot, :, pl.ds(pl.multiple_of(c * lanes, lanes), lanes)] = jnp.broadcast_to(
+                lax.rsqrt(total + 1e-6), (8, lanes)
+            )
+
+    per_part = offs_in.shape[0]
+
+    @pl.loop(0, rows // OFFSET_BLOCK)
+    def _(r):
+        at = pl.ds(pl.multiple_of(r * OFFSET_BLOCK, OFFSET_BLOCK), OFFSET_BLOCK)
+        shift = offs[r // per_part, r % per_part, 0:1, :]
+        pos = (
+            s * block + eh * rows + r * OFFSET_BLOCK
+            + lax.broadcasted_iota(jnp.int32, (OFFSET_BLOCK, lanes), 0) + shift
+        )
+        docs = sdoc[at, :]
+        scale = sscale[at, :]
+        acc = jnp.zeros((OFFSET_BLOCK, lanes), F32)
+
+        def one(slot, acc):
+            for c in range(held // lanes):
+                ct = pl.ds(pl.multiple_of(slot * held + c * lanes, lanes), lanes)
+                cl = pl.ds(c * lanes, lanes)
+                tpos = (
+                    slot * block + el * held + c * lanes
+                    + lax.broadcasted_iota(jnp.int32, (1, lanes), 1)
+                )
+                cosine = kmat[at, ct] * scale * tscale[slot, 0:1, cl]
+                penalty = jnp.where(docs == tdoc[slot, 0:1, cl], 0.0, PENALTY)
+                value = jnp.exp((cosine - penalty) * INV_EPS)
+                value = jnp.where(jnp.abs(tpos - pos) <= BAND, value, 0.0)
+                kmat[at, ct] = value
+                acc = acc + value
+            return acc
+
+        rowacc[at, :] = lax.fori_loop(0, n_seq, one, acc)
+
+    def row_exchange(step):
+        turned = jnp.transpose(rowacc[...])
+        part = turned[0:8]
+        for g in range(1, lanes // 8):
+            part = part + turned[8 * g : 8 * g + 8]
+        rowbuf[step, 0] = part
+        copy = remote(
+            rowbuf.at[step, 0], rowbuf.at[step, 1], row_ssem.at[step], row_rsem.at[step],
+            s, flip(e, 1),
+        )
+        copy.start()
+        copy.wait()
+        return jnp.sum(part + rowbuf[step, 1], axis=0, keepdims=True)
+
+    index = s * 2 + eh
+    peers = 2 * n_seq
+
+    @pl.loop(0, ITERS)
+    def _(step):
+        inverse = 1.0 / row_exchange(step)
+        invrow[...] = jnp.broadcast_to(inverse, invrow.shape)
+        invcol[...] = jnp.transpose(jnp.broadcast_to(inverse, (lanes, rows)))
+
+        @pl.loop(0, n_seq)
+        def _(slot):
+            for c in range(held // lanes):
+                ct = pl.ds(pl.multiple_of(slot * held + c * lanes, lanes), lanes)
+                colpart[slot, :, pl.ds(c * lanes, lanes)] = jnp.sum(
+                    (kmat[:, ct] * invcol[...]).reshape(rows // 8, 8, lanes), axis=0
+                )
+
+        for slot in range(n_seq):
+            colbuf[step, index, slot : slot + 1, :] = jnp.sum(colpart[slot], axis=0, keepdims=True)
+
+        def col_copy(p):
+            to = (index + p) % peers
+            return remote(
+                colbuf.at[step, index], colbuf.at[step, index],
+                col_ssem.at[step, p], col_rsem.at[step, p], to // 2, (to % 2) * 2 + el,
+            )
+
+        @pl.loop(1, peers)
+        def _(p):
+            col_copy(p).start()
+
+        @pl.loop(1, peers)
+        def _(p):
+            owner = (index + peers - p) % peers
+            at = colbuf.at[step, owner]
+            remote(at, at, col_ssem.at[step, 0], col_rsem.at[step, p], s, e).wait_recv()
+
+        total = colbuf[step, 0]
+        for p in range(1, peers):
+            total = total + colbuf[step, p]
+        scal[...] = 1.0 / total
+
+        @pl.loop(1, peers)
+        def _(p):
+            col_copy(p).wait_send()
+
+        @pl.loop(0, rows // 64)
+        def _(r):
+            at = pl.ds(pl.multiple_of(r * 64, 64), 64)
+            acc = jnp.zeros((64, lanes), F32)
+            for slot in range(n_seq):
+                for c in range(held // lanes):
+                    acc = acc + kmat[at, pl.ds(slot * held + c * lanes, lanes)] * (
+                        scal[slot : slot + 1, c * lanes : (c + 1) * lanes]
+                    )
+            rowacc[at, :] = acc
+
+    totals = row_exchange(ITERS)
+    mass[...] = invrow[...] * totals
+    invcol[...] = jnp.transpose(jnp.broadcast_to(1.0 / totals, (lanes, rows)))
+
+    @pl.loop(0, rows // 64)
+    def _(r):
+        at = pl.ds(pl.multiple_of(r * 64, 64), 64)
+        inv = invcol[at, :]
+        for slot in range(n_seq):
+            for c in range(held // lanes):
+                ct = pl.ds(slot * held + c * lanes, lanes)
+                wmat[at, ct] = (
+                    kmat[at, ct] * scal[slot : slot + 1, c * lanes : (c + 1) * lanes] * inv
+                ).astype(BF16)
+
+    copies = []
+    for j in (1, 2, 3, 0):
+        f = flip(e, j)
+
+        @pl.loop(0, rows // 256)
+        def _(r):
+            rt = pl.ds(pl.multiple_of(r * 256, 256), 256)
+            piece[j, rt, :] = jnp.dot(
+                wmat[rt, :], tgt_all[:, cols(f)], preferred_element_type=F32
+            ).astype(BF16)
+
+        if j:
+            copy = remote(piece.at[j], pieces_in.at[j], p_ssem.at[j], p_rsem.at[j], s, f)
+            copy.start()
+            copies.append(copy)
+    for copy in copies:
+        copy.wait_recv()
+    mine = pl.ds(pl.multiple_of(eh * rows, rows), rows)
+    other = pl.ds(pl.multiple_of((1 - eh) * rows, rows), rows)
+    out[mine, :] = (piece[0].astype(F32) + pieces_in[1].astype(F32)).astype(BF16)
+    out[other, :] = (pieces_in[2].astype(F32) + pieces_in[3].astype(F32)).astype(BF16)
+    for copy in copies + sent:
+        copy.wait_send()
+
+
+def fused_device(source, target, doc_ids, offsets):
+    n_seq, n_emb = lax.axis_size("seq"), lax.axis_size("emb")
+    s, e = lax.axis_index("seq"), lax.axis_index("emb")
+    block, feats = source.shape
+    held = rows = block // 2
+    depth = feats * n_emb
+    width = n_seq * held
+    tdoc = lax.dynamic_index_in_dim(doc_ids.reshape(n_seq, 2, held), e % 2, 1, keepdims=False)
+    sdoc = lax.dynamic_slice_in_dim(doc_ids, s * block + (e // 2) * rows, rows, 0)
+    sdoc = jnp.broadcast_to(sdoc[:, None], (rows, 128))
+    tdoc = jnp.broadcast_to(tdoc[:, None], (n_seq, 8, held))
+    offs = jnp.broadcast_to(offsets[:, None, None], (offsets.shape[0], 8, 128))
+    vmem = pl.BlockSpec(memory_space=pltpu.VMEM)
+    dma = pltpu.SemaphoreType.DMA
+    projected, mass = pl.pallas_call(
+        fused_kernel,
+        out_shape=(
+            jax.ShapeDtypeStruct((block, feats), BF16),
+            jax.ShapeDtypeStruct((8, rows), F32),
+        ),
+        in_specs=[vmem] * 5,
+        out_specs=(vmem, vmem),
+        scratch_shapes=[
+            pltpu.VMEM((rows, depth), BF16),
+            pltpu.VMEM((width, depth), BF16),
+            pltpu.VMEM((2, offsets.shape[0], 8, 128), jnp.int32),
+            pltpu.VMEM((rows, width), F32),
+            pltpu.VMEM((rows, width), BF16),
+            pltpu.VMEM((rows, 128), F32),
+            pltpu.VMEM((n_seq, 8, held), F32),
+            pltpu.VMEM((rows, 128), F32),
+            pltpu.VMEM((ITERS + 1, 2, 8, rows), F32),
+            pltpu.VMEM((rows, 128), F32),
+            pltpu.VMEM((8, rows), F32),
+            pltpu.VMEM((n_seq, held), F32),
+            pltpu.VMEM((n_seq, 8, held), F32),
+            pltpu.VMEM((ITERS, 2 * n_seq, n_seq, held), F32),
+            pltpu.VMEM((n_emb, rows, feats), BF16),
+            pltpu.VMEM((n_emb, rows, feats), BF16),
+            dma((3, n_emb)),
+            dma((3, n_emb)),
+            dma((9 * n_emb,)),
+            dma((n_seq, n_emb, 2)),
+            dma((ITERS + 1,)),
+            dma((ITERS + 1,)),
+            dma((ITERS, 2 * n_seq)),
+            dma((ITERS, 2 * n_seq)),
+            dma((n_emb,)),
+            dma((n_emb,)),
+        ],
+        compiler_params=pltpu.CompilerParams(
+            collective_id=0, has_side_effects=True, vmem_limit_bytes=48 << 20
+        ),
+        name="fused_sinkhorn",
+    )(source, target, offs, sdoc, tdoc)
+    row_mass = lax.dynamic_slice_in_dim(mass[0], (e % 2) * (rows // 2), rows // 2, 0)
+    return projected, row_mass
+
+
 def solution(mesh):
     in_specs = (P("seq", "emb"), P("seq", "emb"), P(), P(("seq", "emb")))
     out_specs = (P("seq", "emb"), P(("seq", "emb")))
-    return jax.shard_map(
-        per_device, mesh=mesh, in_specs=in_specs, out_specs=out_specs, check_vma=False
-    )
+
+    def whole(source, target, doc_ids, offsets):
+        n_seq, n_emb = mesh.shape["seq"], mesh.shape["emb"]
+        fits = (n_seq, n_emb) == (8, 4) and source.shape == (8192, 1024)
+        body = fused_device if fits else per_device
+        return jax.shard_map(
+            body, mesh=mesh, in_specs=in_specs, out_specs=out_specs, check_vma=False
+        )(source, target, doc_ids, offsets)
+
+    return whole

time: 969 us -> 142 us (0.15)
  starting transfers between devices: 557 us -> 0 us
  waiting for transfers between devices: 307 us -> 0 us
  Pallas kernels: 0 us -> 135 us
  other arithmetic: 33.3 us -> 0 us
  matrix products: 24.3 us -> 0 us
  blocking collectives: 20.8 us -> 0 us
    ppermute x224 -> x0, starting transfers between devices: 550 us -> none  [shifted_2(): return lax.ppermute(block, axis, route)]
    ppermute x224 -> x0, waiting for transfers between devices: 293 us -> none  [shifted_2(): return lax.ppermute(block, axis, route)]
    pallas_call x0 -> x1, Pallas kernels: none -> 135 us  [fused_device(): pl.pallas_call(fused_kernel, out_shape=(jax.ShapeDtypeStruct((block, feat...]
    reduce_sum x8 -> x0, other arithmetic: 31.7 us -> none  [the longest x2 11.8 us: per_device(): inverse = 1.0 / jnp.sum(kern * scaling[None, :], axis=1)]
    dot_general x2 -> x0, matrix products: 24.3 us -> none  [the longest x1 12.8 us: per_device(): jnp.dot(weights, window, preferred_element_type=jnp.float32)]
    all_to_all x1 -> x0, blocking collectives: 20.8 us -> none  [per_device(): lax.all_to_all(target, 'emb', split_axis=0, concat_axis=1, tiled=True)]
    all_to_all x2 -> x0, waiting for transfers between devices: 13.4 us -> none  [the longest x1 13.4 us: per_device(): lax.all_to_all(mixed, 'emb', split_axis=1, concat_axis=0, tiled=True)]
  transfers between devices with their start and end apart: 226 -> 0, of which waited for: 66 -> 0; matrix products, arithmetic and copies ran while one was open for 1% -> 0% of each run, Pallas kernels for 0% -> 0%
where the time goes in v1:
time: 142 us; the launch traced here: 140 us
  Pallas kernels  135 us (95%)
  local copies, waits for them, and re-layouts  4.09 us (3%)
    pallas_call x1, Pallas kernels, fused_device(): pl.pallas_call(fused_kernel, out_shape=(jax.ShapeDtypeStruct((block, feat...  135 us

profile of v1, /device:TPU:0, one launch (start us, length us, event | category | flops | bytes accessed | tf_op | source)
XLA Modules:
  0.0 139.6 jit_solution(4446509051960844054)
XLA Ops:
  0.6 0.0 copy-start.2
  0.6 0.0 copy-start
  0.7 0.7 copy-done.2
  1.4 0.1 dynamic_slice.12
  1.5 0.7 broadcast_in_dim.8.offs_in
  2.3 0.1 broadcast_in_dim.9.sdoc
  2.4 0.0 copy-done
  2.4 0.0 copy-start.1
  2.4 1.0 copy-done.1
  3.5 134.8 %fused_sinkhorn.1 = (bf16[1024,256]{1,0:T(8,128)(2,1)S(1)}, f32[8,512]{1,0:T(8,128)S(1)}) custom-call(bf16[1024,256]{1,0:T(8,128)(2,1)S(1)} %copy-done, bf16[1024,256]{1,0:T(8,128)(2,1)S(1)} %copy-done.1, s32[4,8,128]{2,1,0:T(8,128)S(1)} %broadcast_in_dim.8.offs_in, s32[512,128]{1,0:T(8,128)S(1)} %broadcast_in_dim.9.sdoc, s32[8,8,512]{2,1,0:T(8,128)S(1)} %broadcast_in_dim.11.tdoc), custom_call_target="tpu_custom_call" | custom-call | tf_op jit(solution)/shard_map/fused_sinkhorn/pallas_call | solution.py:423
  138.3 0.6 constant_dynamic-slice_fusion
  138.8 0.8 copy.10
  (5 shorter events, 0.1 us)
Async XLA Ops:
  0.6 0.8 copy-start.2
  0.6 1.8 %copy-start = (bf16[1024,256]{1,0:T(8,128)(2,1)S(1)}, bf16[1024,256]{1,0:T(8,128)(2,1)}, u32[]{:S(2)}) copy-start(bf16[1024,256]{1,0:T(8,128)(2,1)} %src_in.1) | copy-start | bytes 1572868
  2.4 1.0 copy-start.1

commit v2 on v1

--- a/solution.py
+++ b/solution.py
@@ -120,7 +120,7 @@
 
 def fused_kernel(
     src_in, tgt_in, offs_in, sdoc, tdoc, out, mass,
-    src_all, tgt_all, offs, kmat, wmat, sscale, tscale, rowacc, rowbuf, invcol, invrow, scal, colpart,
+    src_all, tgt_all, offs, kmat, wmat, sscale, tscale, rowacc, rowbuf, invcol, invrow, scal, colpart, tsq,
     colbuf, piece, pieces_in, z_ssem, z_rsem, t_ssem, t_rsem, row_ssem, row_rsem, col_ssem, col_rsem,
     p_ssem, p_rsem,
 ):
@@ -139,12 +139,12 @@
         )
 
     barrier = pltpu.get_barrier_semaphore()
-    for j in range(1, n_emb):
-        pl.semaphore_signal(barrier, inc=1, device_id=(s, flip(e, j)), device_id_type=MESH)
-    for k in range(1, n_seq):
-        pl.semaphore_signal(barrier, inc=1, device_id=(flip(s, k), e), device_id_type=MESH)
-        pl.semaphore_signal(barrier, inc=1, device_id=(flip(s, k), flip(e, 2)), device_id_type=MESH)
-    pl.semaphore_wait(barrier, n_emb - 1 + 2 * (n_seq - 1))
+    met = [(0, 1), (0, 2), (0, 3), (1, 0), (2, 0), (4, 0), (6, 0), (1, 2)]
+    for k, j in met:
+        pl.semaphore_signal(
+            barrier, inc=1, device_id=(flip(s, k), flip(e, j)), device_id_type=MESH
+        )
+    pl.semaphore_wait(barrier, len(met))
 
     def cols(f):
         return pl.ds(pl.multiple_of(f * feats, feats), feats)
@@ -159,22 +159,35 @@
         sent.append(copy)
 
     mine_t = pl.ds(pl.multiple_of(s * held, held), held)
+    inner = ((e + 1) // 2) % 2
+
+    def src_part(part):
+        return src_in.at[pl.ds(pl.multiple_of(part * rows, rows), rows), :]
+
+    start(remote(
+        src_part(1 - eh), src_all.at[:, cols(e)], z_ssem.at[1, 2], z_rsem.at[1, 2 + inner], s, 2 - eh,
+    ))
     for j in range(1, n_emb):
         peer = flip(e, j)
         start(remote(
             tgt_in.at[pl.ds(pl.multiple_of((peer % 2) * held, held), held), :],
             tgt_all.at[mine_t, cols(e)], z_ssem.at[0, j], z_rsem.at[0, j], s, peer,
         ))
+    start(remote(
+        src_part(eh), src_all.at[:, cols(e)], z_ssem.at[1, 1], z_rsem.at[1, 1], s, flip(e, 1),
+    ))
     start(remote(offs_in, offs.at[el], z_ssem.at[2, 0], z_rsem.at[2, 0], s, flip(e, 1)))
-    for j in range(1, n_emb):
-        peer = flip(e, j)
-        start(remote(
-            src_in.at[pl.ds(pl.multiple_of((peer // 2) * rows, rows), rows), :],
-            src_all.at[:, cols(e)], z_ssem.at[1, j], z_rsem.at[1, j], s, peer,
-        ))
     tgt_all[mine_t, cols(e)] = tgt_in[pl.ds(pl.multiple_of(el * held, held), held), :]
     src_all[:, cols(e)] = src_in[pl.ds(pl.multiple_of(eh * rows, rows), rows), :]
     offs[el] = offs_in[...]
+
+    def src_arrived(j):
+        at = src_all.at[:, cols(flip(e, j))]
+        remote(at, at, z_ssem.at[1, 0], z_rsem.at[1, j], s, e).wait_recv()
+
+    def handed_on(j):
+        at = src_all.at[:, cols(flip(e, j))]
+        return remote(at, at, z_ssem.at[2, j], z_rsem.at[1, 5 - j], s, flip(e, 1))
 
     count = [0]
 
@@ -208,60 +221,86 @@
             arrived(6, j, part * half, half, part)
             send(flip(s, 6), j, 7, 1, part * half, half, part)
 
-    for step in range(n_emb + 2):
-        for stage, lag in ((first, 0), (second, 1), (third, 2)):
-            if 0 <= step - lag < n_emb:
-                stage(step - lag)
-
-    for j in range(1, n_emb):
-        at = src_all.at[:, cols(flip(e, j))]
-        remote(at, at, z_ssem.at[1, 0], z_rsem.at[1, j], s, e).wait_recv()
-    at = offs.at[1 - el]
-    remote(at, at, z_ssem.at[2, 0], z_rsem.at[2, 0], s, e).wait_recv()
-
     lanes = 128
     depth = src_all.shape[1]
 
-    @pl.loop(0, rows // 64)
-    def _(r):
-        at = pl.ds(pl.multiple_of(r * 64, 64), 64)
-        acc = jnp.zeros((64, lanes), F32)
-        for c in range(depth // lanes):
-            x = src_all[at, pl.ds(c * lanes, lanes)].astype(F32)
-            acc = acc + x * x
-        total = jnp.sum(acc, axis=1, keepdims=True)
-        sscale[at, :] = jnp.broadcast_to(lax.rsqrt(total + 1e-6), (64, lanes))
-
-    for j in range(n_emb):
+    def fourth(j):
         for k in (1, 3, 5):
             arrived(k, j)
         for part in range(2):
             arrived(7, j, part * half, half, part)
-
-    @pl.loop(0, n_seq)
-    def _(slot):
-        base = slot * held
-        at = pl.ds(pl.multiple_of(base, held), held)
-
-        @pl.loop(0, rows // 256)
+        if j == 1:
+            src_arrived(1)
+        elif j:
+            @pl.when(inner == 0)
+            def _():
+                src_arrived(j)
+
+        f = flip(e, j)
+
+        def squares(ref, at):
+            acc = None
+            for c in range(feats // lanes):
+                ct = pl.ds(pl.multiple_of(f * feats + c * lanes, lanes), lanes)
+                x = ref[at, ct].astype(F32)
+                acc = x * x if acc is None else acc + x * x
+            return acc
+
+        @pl.loop(0, rows // 64)
         def _(r):
-            rt = pl.ds(pl.multiple_of(r * 256, 256), 256)
-            kmat[rt, at] = lax.dot_general(
-                src_all[rt, :], tgt_all[at, :], (((1,), (1,)), ((), ())),
-                preferred_element_type=F32,
-            )
-
-        @pl.loop(0, held // lanes)
-        def _(c):
-            tt = pl.ds(pl.multiple_of(base + c * lanes, lanes), lanes)
-            acc = jnp.zeros((lanes, lanes), F32)
-            for d in range(depth // lanes):
-                x = tgt_all[tt, pl.ds(d * lanes, lanes)].astype(F32)
-                acc = acc + x * x
-            total = jnp.sum(jnp.transpose(acc), axis=0, keepdims=True)
-            tscale[slot, :, pl.ds(pl.multiple_of(c * lanes, lanes), lanes)] = jnp.broadcast_to(
-                lax.rsqrt(total + 1e-6), (8, lanes)
-            )
+            at = pl.ds(pl.multiple_of(r * 64, 64), 64)
+            total = squares(src_all, at)
+            if j:
+                total = total + sscale[at, :]
+            if j == n_emb - 1:
+                total = jnp.sum(total, axis=1, keepdims=True)
+                total = jnp.broadcast_to(lax.rsqrt(total + 1e-6), (64, lanes))
+            sscale[at, :] = total
+
+        @pl.loop(0, n_seq)
+        def _(slot):
+            base = slot * held
+            at = pl.ds(pl.multiple_of(base, held), held)
+
+            @pl.loop(0, rows // 256)
+            def _(r):
+                rt = pl.ds(pl.multiple_of(r * 256, 256), 256)
+                dots = lax.dot_general(
+                    src_all[rt, cols(f)], tgt_all[at, cols(f)], (((1,), (1,)), ((), ())),
+                    preferred_element_type=F32,
+                )
+                kmat[rt, at] = kmat[rt, at] + dots if j else dots
+
+            for c in range(held // lanes):
+                tt = pl.ds(pl.multiple_of(base + c * lanes, lanes), lanes)
+                acc = squares(tgt_all, tt)
+                if j:
+                    acc = acc + tsq[tt, :]
+                if j < n_emb - 1:
+                    tsq[tt, :] = acc
+                else:
+                    total = jnp.sum(jnp.transpose(acc), axis=0, keepdims=True)
+                    tscale[slot, :, pl.ds(c * lanes, lanes)] = jnp.broadcast_to(
+                        lax.rsqrt(total + 1e-6), (8, lanes)
+                    )
+
+    first(0)
+
+    @pl.when(inner == 1)
+    def _():
+        for j in (2, 3):
+            src_arrived(j)
+            handed_on(j).start()
+
+    for j in range(1, n_emb + 1):
+        if j < n_emb:
+            first(j)
+        second(j - 1)
+        third(j - 1)
+        fourth(j - 1)
+
+    at = offs.at[1 - el]
+    remote(at, at, z_ssem.at[2, 0], z_rsem.at[2, 0], s, e).wait_recv()
 
     per_part = offs_in.shape[0]
 
@@ -295,7 +334,7 @@
 
         rowacc[at, :] = lax.fori_loop(0, n_seq, one, acc)
 
-    def row_exchange(step):
+    def row_start(step):
         turned = jnp.transpose(rowacc[...])
         part = turned[0:8]
         for g in range(1, lanes // 8):
@@ -306,15 +345,29 @@
             s, flip(e, 1),
         )
         copy.start()
+        return copy
+
+    def row_finish(step, copy):
         copy.wait()
-        return jnp.sum(part + rowbuf[step, 1], axis=0, keepdims=True)
-
-    index = s * 2 + eh
-    peers = 2 * n_seq
-
-    @pl.loop(0, ITERS)
-    def _(step):
-        inverse = 1.0 / row_exchange(step)
+        return jnp.sum(rowbuf[step, 0] + rowbuf[step, 1], axis=0, keepdims=True)
+
+    def exchange(step, level, value, route):
+        colbuf[step, level, 0] = value
+        copies = []
+        for p, (k, j) in enumerate(route, 1):
+            copies.append(remote(
+                colbuf.at[step, level, 0], colbuf.at[step, level, p],
+                col_ssem.at[step, level, p], col_rsem.at[step, level, p], flip(s, k), flip(e, j),
+            ))
+            copies[-1].start()
+        total = value
+        for p, copy in enumerate(copies, 1):
+            copy.wait()
+            total = total + colbuf[step, level, p]
+        return total
+
+    def iterate(step):
+        inverse = 1.0 / row_finish(step, row_start(step))
         invrow[...] = jnp.broadcast_to(inverse, invrow.shape)
         invcol[...] = jnp.transpose(jnp.broadcast_to(inverse, (lanes, rows)))
 
@@ -327,70 +380,59 @@
                 )
 
         for slot in range(n_seq):
-            colbuf[step, index, slot : slot + 1, :] = jnp.sum(colpart[slot], axis=0, keepdims=True)
-
-        def col_copy(p):
-            to = (index + p) % peers
-            return remote(
-                colbuf.at[step, index], colbuf.at[step, index],
-                col_ssem.at[step, p], col_rsem.at[step, p], to // 2, (to % 2) * 2 + el,
-            )
-
-        @pl.loop(1, peers)
-        def _(p):
-            col_copy(p).start()
-
-        @pl.loop(1, peers)
-        def _(p):
-            owner = (index + peers - p) % peers
-            at = colbuf.at[step, owner]
-            remote(at, at, col_ssem.at[step, 0], col_rsem.at[step, p], s, e).wait_recv()
-
-        total = colbuf[step, 0]
-        for p in range(1, peers):
-            total = total + colbuf[step, p]
-        scal[...] = 1.0 / total
-
-        @pl.loop(1, peers)
-        def _(p):
-            col_copy(p).wait_send()
-
+            scal[slot : slot + 1, :] = jnp.sum(colpart[slot], axis=0, keepdims=True)
+        total = exchange(step, 0, scal[...], [(1, 0), (0, 2), (1, 2)])
+        scal[...] = 1.0 / exchange(step, 1, total, [(2, 0), (4, 0), (6, 0)])
+
+    def row_sums(last):
         @pl.loop(0, rows // 64)
         def _(r):
             at = pl.ds(pl.multiple_of(r * 64, 64), 64)
             acc = jnp.zeros((64, lanes), F32)
             for slot in range(n_seq):
                 for c in range(held // lanes):
-                    acc = acc + kmat[at, pl.ds(slot * held + c * lanes, lanes)] * (
-                        scal[slot : slot + 1, c * lanes : (c + 1) * lanes]
-                    )
+                    ct = pl.ds(slot * held + c * lanes, lanes)
+                    scaled = kmat[at, ct] * scal[slot : slot + 1, c * lanes : (c + 1) * lanes]
+                    acc = acc + scaled
+                    if last:
+                        wmat[at, ct] = scaled.astype(BF16)
             rowacc[at, :] = acc
 
-    totals = row_exchange(ITERS)
-    mass[...] = invrow[...] * totals
-    invcol[...] = jnp.transpose(jnp.broadcast_to(1.0 / totals, (lanes, rows)))
-
-    @pl.loop(0, rows // 64)
-    def _(r):
-        at = pl.ds(pl.multiple_of(r * 64, 64), 64)
-        inv = invcol[at, :]
-        for slot in range(n_seq):
-            for c in range(held // lanes):
-                ct = pl.ds(slot * held + c * lanes, lanes)
-                wmat[at, ct] = (
-                    kmat[at, ct] * scal[slot : slot + 1, c * lanes : (c + 1) * lanes] * inv
-                ).astype(BF16)
-
+    @pl.loop(0, ITERS - 1)
+    def _(step):
+        iterate(step)
+        row_sums(False)
+
+    iterate(ITERS - 1)
+    row_sums(True)
+
+    totals_copy = row_start(ITERS)
     copies = []
-    for j in (1, 2, 3, 0):
+    for j in (3, 2, 1, 0):
         f = flip(e, j)
+        early = j == 3
+
+        def product(rt):
+            return jnp.dot(wmat[rt, :], tgt_all[:, cols(f)], preferred_element_type=F32)
+
+        if early:
+            @pl.loop(0, rows // 256)
+            def _(r):
+                rt = pl.ds(pl.multiple_of(r * 256, 256), 256)
+                kmat[rt, 0:feats] = product(rt)
+
+            totals = row_finish(ITERS, totals_copy)
+            mass[...] = invrow[...] * totals
+            invcol[...] = jnp.transpose(jnp.broadcast_to(1.0 / totals, (lanes, rows)))
 
         @pl.loop(0, rows // 256)
         def _(r):
             rt = pl.ds(pl.multiple_of(r * 256, 256), 256)
-            piece[j, rt, :] = jnp.dot(
-                wmat[rt, :], tgt_all[:, cols(f)], preferred_element_type=F32
-            ).astype(BF16)
+            mixed = kmat[rt, 0:feats] if early else product(rt)
+            inv = invcol[rt, :]
+            for c in range(feats // lanes):
+                cl = slice(c * lanes, (c + 1) * lanes)
+                piece[j, rt, cl] = (mixed[:, cl] * inv).astype(BF16)
 
         if j:
             copy = remote(piece.at[j], pieces_in.at[j], p_ssem.at[j], p_rsem.at[j], s, f)
@@ -404,6 +446,11 @@
     out[other, :] = (pieces_in[2].astype(F32) + pieces_in[3].astype(F32)).astype(BF16)
     for copy in copies + sent:
         copy.wait_send()
+
+    @pl.when(inner == 1)
+    def _():
+        for j in (2, 3):
+            handed_on(j).wait_send()
 
 
 def fused_device(source, target, doc_ids, offsets):
@@ -442,7 +489,8 @@
             pltpu.VMEM((8, rows), F32),
             pltpu.VMEM((n_seq, held), F32),
             pltpu.VMEM((n_seq, 8, held), F32),
-            pltpu.VMEM((ITERS, 2 * n_seq, n_seq, held), F32),
+            pltpu.VMEM((width, 128), F32),
+            pltpu.VMEM((ITERS, 2, 4, n_seq, held), F32),
             pltpu.VMEM((n_emb, rows, feats), BF16),
             pltpu.VMEM((n_emb, rows, feats), BF16),
             dma((3, n_emb)),
@@ -451,8 +499,8 @@
             dma((n_seq, n_emb, 2)),
             dma((ITERS + 1,)),
             dma((ITERS + 1,)),
-            dma((ITERS, 2 * n_seq)),
-            dma((ITERS, 2 * n_seq)),
+            dma((ITERS, 2, 4)),
+            dma((ITERS, 2, 4)),
             dma((n_emb,)),
             dma((n_emb,)),
         ],

time: 142 us -> 152 us (1.070); the launches traced: 140 us -> 152 us
  Pallas kernels: 135 us -> 147 us
    pallas_call x1, Pallas kernels: 135 us -> 147 us  [fused_device(): pl.pallas_call(fused_kernel, out_shape=(jax.ShapeDtypeStruct((block, feat...]
where the time goes in v2:
time: 152 us
  Pallas kernels  147 us (97%)
  local copies, waits for them, and re-layouts  4.09 us (3%)
    pallas_call x1, Pallas kernels, fused_device(): pl.pallas_call(fused_kernel, out_shape=(jax.ShapeDtypeStruct((block, feat...  147 us

profile of v2, /device:TPU:0, one launch (start us, length us, event | category | flops | bytes accessed | tf_op | source)
XLA Modules:
  0.0 152.3 jit_solution(1496786054201493907)
XLA Ops:
  0.6 0.0 copy-start.2
  0.6 0.0 copy-start
  0.7 0.7 copy-done.2
  1.4 0.1 dynamic_slice.12
  1.5 0.7 broadcast_in_dim.8.offs_in
  2.3 0.1 broadcast_in_dim.9.sdoc
  2.4 0.0 copy-done
  2.4 0.0 copy-start.1
  2.4 1.0 copy-done.1
  3.5 147.4 %fused_sinkhorn.1 = (bf16[1024,256]{1,0:T(8,128)(2,1)S(1)}, f32[8,512]{1,0:T(8,128)S(1)}) custom-call(bf16[1024,256]{1,0:T(8,128)(2,1)S(1)} %copy-done, bf16[1024,256]{1,0:T(8,128)(2,1)S(1)} %copy-done.1, s32[4,8,128]{2,1,0:T(8,128)S(1)} %broadcast_in_dim.8.offs_in, s32[512,128]{1,0:T(8,128)S(1)} %broadcast_in_dim.9.sdoc, s32[8,8,512]{2,1,0:T(8,128)S(1)} %broadcast_in_dim.11.tdoc), custom_call_target="tpu_custom_call" | custom-call | tf_op jit(solution)/shard_map/fused_sinkhorn/pallas_call | solution.py:470
  150.9 0.6 constant_dynamic-slice_fusion
  151.5 0.8 copy.10
  (5 shorter events, 0.1 us)
Async XLA Ops:
  0.6 0.8 copy-start.2
  0.6 1.8 %copy-start = (bf16[1024,256]{1,0:T(8,128)(2,1)S(1)}, bf16[1024,256]{1,0:T(8,128)(2,1)}, u32[]{:S(2)}) copy-start(bf16[1024,256]{1,0:T(8,128)(2,1)} %src_in.1) | copy-start | bytes 1572868
  2.4 1.0 copy-start.1

commit v3 on v2

--- a/solution.py
+++ b/solution.py
@@ -120,7 +120,7 @@
 
 def fused_kernel(
     src_in, tgt_in, offs_in, sdoc, tdoc, out, mass,
-    src_all, tgt_all, offs, kmat, wmat, sscale, tscale, rowacc, rowbuf, invcol, invrow, scal, colpart, tsq,
+    src_all, tgt_all, offs, kmat, wmat, sscale, tscale, rowacc, rowbuf, invcol, invrow, scal, colpart,
     colbuf, piece, pieces_in, z_ssem, z_rsem, t_ssem, t_rsem, row_ssem, row_rsem, col_ssem, col_rsem,
     p_ssem, p_rsem,
 ):
@@ -128,7 +128,7 @@
     s, e = lax.axis_index("seq"), lax.axis_index("emb")
     eh, el = e // 2, e % 2
     block, feats = src_in.shape
-    rows = src_all.shape[0]
+    rows = src_all.shape[1]
     held = block // 2
     half = held // 2
 
@@ -146,11 +146,8 @@
         )
     pl.semaphore_wait(barrier, len(met))
 
-    def cols(f):
-        return pl.ds(pl.multiple_of(f * feats, feats), feats)
-
     def region(slot, j, start=0, count=held):
-        return tgt_all.at[pl.ds(pl.multiple_of(slot * held + start, half), count), cols(flip(e, j))]
+        return tgt_all.at[flip(e, j), pl.ds(pl.multiple_of(slot * held + start, half), count), :]
 
     sent = []
 
@@ -159,35 +156,29 @@
         sent.append(copy)
 
     mine_t = pl.ds(pl.multiple_of(s * held, held), held)
-    inner = ((e + 1) // 2) % 2
 
     def src_part(part):
         return src_in.at[pl.ds(pl.multiple_of(part * rows, rows), rows), :]
 
-    start(remote(
-        src_part(1 - eh), src_all.at[:, cols(e)], z_ssem.at[1, 2], z_rsem.at[1, 2 + inner], s, 2 - eh,
-    ))
     for j in range(1, n_emb):
         peer = flip(e, j)
         start(remote(
             tgt_in.at[pl.ds(pl.multiple_of((peer % 2) * held, held), held), :],
-            tgt_all.at[mine_t, cols(e)], z_ssem.at[0, j], z_rsem.at[0, j], s, peer,
+            tgt_all.at[e, mine_t, :], z_ssem.at[0, j], z_rsem.at[0, j], s, peer,
         ))
-    start(remote(
-        src_part(eh), src_all.at[:, cols(e)], z_ssem.at[1, 1], z_rsem.at[1, 1], s, flip(e, 1),
-    ))
+    for j in range(1, n_emb):
+        peer = flip(e, j)
+        start(remote(
+            src_part(peer // 2), src_all.at[e], z_ssem.at[1, j], z_rsem.at[1, j], s, peer,
+        ))
     start(remote(offs_in, offs.at[el], z_ssem.at[2, 0], z_rsem.at[2, 0], s, flip(e, 1)))
-    tgt_all[mine_t, cols(e)] = tgt_in[pl.ds(pl.multiple_of(el * held, held), held), :]
-    src_all[:, cols(e)] = src_in[pl.ds(pl.multiple_of(eh * rows, rows), rows), :]
+    tgt_all[e, mine_t, :] = tgt_in[pl.ds(pl.multiple_of(el * held, held), held), :]
+    src_all[e] = src_in[pl.ds(pl.multiple_of(eh * rows, rows), rows), :]
     offs[el] = offs_in[...]
 
     def src_arrived(j):
-        at = src_all.at[:, cols(flip(e, j))]
+        at = src_all.at[flip(e, j)]
         remote(at, at, z_ssem.at[1, 0], z_rsem.at[1, j], s, e).wait_recv()
-
-    def handed_on(j):
-        at = src_all.at[:, cols(flip(e, j))]
-        return remote(at, at, z_ssem.at[2, j], z_rsem.at[1, 5 - j], s, flip(e, 1))
 
     count = [0]
 
@@ -222,82 +213,60 @@
             send(flip(s, 6), j, 7, 1, part * half, half, part)
 
     lanes = 128
-    depth = src_all.shape[1]
-
-    def fourth(j):
+
+    for step in range(n_emb + 2):
+        for stage, lag in ((first, 0), (second, 1), (third, 2)):
+            if 0 <= step - lag < n_emb:
+                stage(step - lag)
+
+    def squares(ref, at):
+        acc = jnp.zeros((at.size, lanes), F32)
+        for f in range(n_emb):
+            for c in range(feats // lanes):
+                x = ref[f, at, pl.ds(c * lanes, lanes)].astype(F32)
+                acc = acc + x * x
+        return acc
+
+    for j in range(n_emb):
         for k in (1, 3, 5):
             arrived(k, j)
         for part in range(2):
             arrived(7, j, part * half, half, part)
-        if j == 1:
-            src_arrived(1)
-        elif j:
-            @pl.when(inner == 0)
-            def _():
-                src_arrived(j)
-
-        f = flip(e, j)
-
-        def squares(ref, at):
-            acc = None
-            for c in range(feats // lanes):
-                ct = pl.ds(pl.multiple_of(f * feats + c * lanes, lanes), lanes)
-                x = ref[at, ct].astype(F32)
-                acc = x * x if acc is None else acc + x * x
-            return acc
-
-        @pl.loop(0, rows // 64)
+
+    @pl.loop(0, n_seq)
+    def _(slot):
+        @pl.loop(0, held // lanes)
+        def _(c):
+            tt = pl.ds(pl.multiple_of(slot * held + c * lanes, lanes), lanes)
+            total = jnp.sum(jnp.transpose(squares(tgt_all, tt)), axis=0, keepdims=True)
+            tscale[slot, :, pl.ds(pl.multiple_of(c * lanes, lanes), lanes)] = jnp.broadcast_to(
+                lax.rsqrt(total + 1e-6), (8, lanes)
+            )
+
+    for j in range(1, n_emb):
+        src_arrived(j)
+
+    @pl.loop(0, rows // 64)
+    def _(r):
+        at = pl.ds(pl.multiple_of(r * 64, 64), 64)
+        total = jnp.sum(squares(src_all, at), axis=1, keepdims=True)
+        sscale[at, :] = jnp.broadcast_to(lax.rsqrt(total + 1e-6), (64, lanes))
+
+    @pl.loop(0, n_seq)
+    def _(slot):
+        at = pl.ds(pl.multiple_of(slot * held, held), held)
+
+        @pl.loop(0, rows // 256)
         def _(r):
-            at = pl.ds(pl.multiple_of(r * 64, 64), 64)
-            total = squares(src_all, at)
-            if j:
-                total = total + sscale[at, :]
-            if j == n_emb - 1:
-                total = jnp.sum(total, axis=1, keepdims=True)
-                total = jnp.broadcast_to(lax.rsqrt(total + 1e-6), (64, lanes))
-            sscale[at, :] = total
-
-        @pl.loop(0, n_seq)
-        def _(slot):
-            base = slot * held
-            at = pl.ds(pl.multiple_of(base, held), held)
-
-            @pl.loop(0, rows // 256)
-            def _(r):
-                rt = pl.ds(pl.multiple_of(r * 256, 256), 256)
-                dots = lax.dot_general(
-                    src_all[rt, cols(f)], tgt_all[at, cols(f)], (((1,), (1,)), ((), ())),
+            rt = pl.ds(pl.multiple_of(r * 256, 256), 256)
+            dots = None
+            for f in range(n_emb):
+                dot = lax.dot_general(
+                    src_all[f, rt, :], tgt_all[f, at, :], (((1,), (1,)), ((), ())),
                     preferred_element_type=F32,
                 )
-                kmat[rt, at] = kmat[rt, at] + dots if j else dots
-
-            for c in range(held // lanes):
-                tt = pl.ds(pl.multiple_of(base + c * lanes, lanes), lanes)
-                acc = squares(tgt_all, tt)
-                if j:
-                    acc = acc + tsq[tt, :]
-                if j < n_emb - 1:
-                    tsq[tt, :] = acc
-                else:
-                    total = jnp.sum(jnp.transpose(acc), axis=0, keepdims=True)
-                    tscale[slot, :, pl.ds(c * lanes, lanes)] = jnp.broadcast_to(
-                        lax.rsqrt(total + 1e-6), (8, lanes)
-                    )
-
-    first(0)
-
-    @pl.when(inner == 1)
-    def _():
-        for j in (2, 3):
-            src_arrived(j)
-            handed_on(j).start()
-
-    for j in range(1, n_emb + 1):
-        if j < n_emb:
-            first(j)
-        second(j - 1)
-        third(j - 1)
-        fourth(j - 1)
+                dots = dot if dots is None else dots + dot
+            kmat[rt, at] = dots
 
     at = offs.at[1 - el]
     remote(at, at, z_ssem.at[2, 0], z_rsem.at[2, 0], s, e).wait_recv()
@@ -413,7 +382,7 @@
         early = j == 3
 
         def product(rt):
-            return jnp.dot(wmat[rt, :], tgt_all[:, cols(f)], preferred_element_type=F32)
+            return jnp.dot(wmat[rt, :], tgt_all[f], preferred_element_type=F32)
 
         if early:
             @pl.loop(0, rows // 256)
@@ -447,18 +416,12 @@
     for copy in copies + sent:
         copy.wait_send()
 
-    @pl.when(inner == 1)
-    def _():
-        for j in (2, 3):
-            handed_on(j).wait_send()
-
 
 def fused_device(source, target, doc_ids, offsets):
     n_seq, n_emb = lax.axis_size("seq"), lax.axis_size("emb")
     s, e = lax.axis_index("seq"), lax.axis_index("emb")
     block, feats = source.shape
     held = rows = block // 2
-    depth = feats * n_emb
     width = n_seq * held
     tdoc = lax.dynamic_index_in_dim(doc_ids.reshape(n_seq, 2, held), e % 2, 1, keepdims=False)
     sdoc = lax.dynamic_slice_in_dim(doc_ids, s * block + (e // 2) * rows, rows, 0)
@@ -476,8 +439,8 @@
         in_specs=[vmem] * 5,
         out_specs=(vmem, vmem),
         scratch_shapes=[
-            pltpu.VMEM((rows, depth), BF16),
-            pltpu.VMEM((width, depth), BF16),
+            pltpu.VMEM((n_emb, rows, feats), BF16),
+            pltpu.VMEM((n_emb, width, feats), BF16),
             pltpu.VMEM((2, offsets.shape[0], 8, 128), jnp.int32),
             pltpu.VMEM((rows, width), F32),
             pltpu.VMEM((rows, width), BF16),
@@ -489,7 +452,6 @@
             pltpu.VMEM((8, rows), F32),
             pltpu.VMEM((n_seq, held), F32),
             pltpu.VMEM((n_seq, 8, held), F32),
-            pltpu.VMEM((width, 128), F32),
             pltpu.VMEM((ITERS, 2, 4, n_seq, held), F32),
             pltpu.VMEM((n_emb, rows, feats), BF16),
             pltpu.VMEM((n_emb, rows, feats), BF16),

time: 152 us -> 137 us (0.901)
  Pallas kernels: 147 us -> 132 us
    pallas_call x1, Pallas kernels: 147 us -> 132 us  [fused_device(): pl.pallas_call(fused_kernel, out_shape=(jax.ShapeDtypeStruct((block, feat...]
where the time goes in v3:
time: 137 us
  Pallas kernels  132 us (96%)
  local copies, waits for them, and re-layouts  4.09 us (3%)
    pallas_call x1, Pallas kernels, fused_device(): pl.pallas_call(fused_kernel, out_shape=(jax.ShapeDtypeStruct((block, feat...  132 us

profile of v3, /device:TPU:0, one launch (start us, length us, event | category | flops | bytes accessed | tf_op | source)
XLA Modules:
  0.0 136.7 jit_solution(5415875950296575740)
XLA Ops:
  0.6 0.0 copy-start.2
  0.6 0.0 copy-start
  0.7 0.7 copy-done.2
  1.4 0.1 dynamic_slice.12
  1.5 0.7 broadcast_in_dim.8.offs_in
  2.3 0.1 broadcast_in_dim.9.sdoc
  2.4 0.0 copy-done
  2.4 0.0 copy-start.1
  2.4 1.0 copy-done.1
  3.5 131.9 %fused_sinkhorn.1 = (bf16[1024,256]{1,0:T(8,128)(2,1)S(1)}, f32[8,512]{1,0:T(8,128)S(1)}) custom-call(bf16[1024,256]{1,0:T(8,128)(2,1)S(1)} %copy-done, bf16[1024,256]{1,0:T(8,128)(2,1)S(1)} %copy-done.1, s32[4,8,128]{2,1,0:T(8,128)S(1)} %broadcast_in_dim.8.offs_in, s32[512,128]{1,0:T(8,128)S(1)} %broadcast_in_dim.9.sdoc, s32[8,8,512]{2,1,0:T(8,128)S(1)} %broadcast_in_dim.11.tdoc), custom_call_target="tpu_custom_call" | custom-call | tf_op jit(solution)/shard_map/fused_sinkhorn/pallas_call | solution.py:433
  135.4 0.6 constant_dynamic-slice_fusion
  135.9 0.8 copy.10
  (5 shorter events, 0.1 us)
Async XLA Ops:
  0.6 0.8 copy-start.2
  0.6 1.8 %copy-start = (bf16[1024,256]{1,0:T(8,128)(2,1)S(1)}, bf16[1024,256]{1,0:T(8,128)(2,1)}, u32[]{:S(2)}) copy-start(bf16[1024,256]{1,0:T(8,128)(2,1)} %src_in.1) | copy-start | bytes 1572868
  2.4 1.0 copy-start.1
